TPU v7x, 32 devices: a whole 2x2x4 slice. The times are simulated.
32 devices in a mesh: tok: 8 (over z, y), mdl: 4 (over x, core).
Axes of the slice: x: 2, y: 2, z: 4, core: 2. Of those that a mesh axis runs over, the one named last changes fastest.
Arguments:
- tokens: bfloat16 [2048, 5120], P('tok'), may hold values from -32 to 32
- norm_gain: bfloat16 [5120], replicated, may hold values from 0.099609375 to 1.8984375
- w_query: bfloat16 [5120, 4096], P(None, 'mdl'), may hold values from -0.078125 to 0.078125
- w_key: bfloat16 [5120, 1024], P(None, 'mdl'), may hold values from -0.3125 to 0.3125
- w_value: bfloat16 [5120, 1024], P(None, 'mdl'), may hold values from -0.078125 to 0.078125
- w_out: bfloat16 [4096, 5120], P('mdl'), may hold values from -0.09375 to 0.09375
- prompt_keys: bfloat16 [6, 4096, 8, 128], P(None, 'tok', 'mdl'), may hold values from -6 to 6
- prompt_values: bfloat16 [6, 4096, 8, 128], P(None, 'tok', 'mdl'), may hold values from -24 to 24
- cache_keys: bfloat16 [64, 2048, 8, 128], P('tok', None, 'mdl'), may hold values from -6 to 6
- cache_values: bfloat16 [64, 2048, 8, 128], P('tok', None, 'mdl'), may hold values from -24 to 24
- cache_length: int32 [64], P('tok'), may hold values from 1 to 2048, as said below
- request_group: int32 [64], replicated, may hold values from 0 to 5
- ancestors: int32 [64, 32, 32], P('tok'), may hold values from 0 to 1, as said below
- accepted: int32 [64, 8], P('tok'), may hold values from -1 to 31, as said below
Outputs:
- attention_out: bfloat16 [2048, 5120], P('tok', 'mdl')
- compact_rows: bfloat16 [64, 8, 5120], P('tok', None, 'mdl')
Inputs may be any that keep to these rules, and one draw needn't show every extreme that they name: `cache_length`: some request has exactly 2048 live slots. ancestors[r, a, b] is 1 where tree slot b is slot a itself or an ancestor of it in request r's draft tree, else 0; each tree has one root, and slots are in no particular order. Entry k of request r is the tree slot of the accepted path's node at depth k, from the root on, for k below the path's length, and -1 after it; a path holds 1 to 8 nodes, and some request's path holds 8.
All inputs are finite; a program needn't handle non-finite values.
Results may differ from a plain program's by a relative error of at most 0.017.
Values may be sent and summed in bfloat16 or wider, within the bound.
A program may use at most 192 MiB of HBM per device.

v0:
```python
import jax
import jax.numpy as jnp
from jax import lax
from jax.sharding import PartitionSpec as P

PROMPT = 4096


THETA = 100000000.0
EPS = 1e-05


def rotate_pairs(vectors, positions):
    middle = vectors.shape[-1] // 2
    exponent = jnp.arange(middle, dtype=jnp.float32) * (2.0 / vectors.shape[-1])
    inverse = jnp.power(jnp.float32(THETA), -exponent)
    angles = positions.astype(jnp.float32)[:, None] * inverse[None, :]
    cosine = jnp.cos(angles)[:, None, :]
    sine_part = jnp.sin(angles)[:, None, :]
    leading = vectors[..., :middle]
    trailing = vectors[..., middle:]
    return jnp.concatenate(
        [leading * cosine - trailing * sine_part, trailing * cosine + leading * sine_part], axis=-1
    )


def slice_attention(grouped, chosen_keys, chosen_values, slice_rows, factor):
    pieces = chosen_keys.shape[1] // slice_rows
    layout = (chosen_keys.shape[0], pieces, slice_rows, chosen_keys.shape[2], chosen_keys.shape[3])
    keys_split = chosen_keys.reshape(layout)
    values_split = chosen_values.reshape(layout)
    scores = (
        jnp.einsum("ntkgd,nsckd->ntkgsc", grouped, keys_split, preferred_element_type=jnp.float32)
        * factor
    )
    weights = jnp.exp(scores)
    totals = jnp.sum(weights, axis=5)
    numerator = jnp.einsum(
        "ntkgsc,nsckd->ntkgsd",
        weights.astype(jnp.bfloat16),
        values_split,
        preferred_element_type=jnp.float32,
    )
    outputs = (numerator / totals[..., None]).astype(jnp.bfloat16)
    return (outputs, totals)


def cache_block(grouped, key_block, value_block, lengths, factor):
    scores = (
        jnp.einsum("ntkgd,nckd->ntkgc", grouped, key_block, preferred_element_type=jnp.float32)
        * factor
    )
    places = jnp.arange(key_block.shape[1], dtype=jnp.int32)
    live = places[None, :] < lengths[:, None]
    weights = jnp.where(live[:, None, None, None, :], jnp.exp(scores), 0.0)
    numerator = jnp.einsum(
        "ntkgc,nckd->ntkgd",
        weights.astype(jnp.bfloat16),
        value_block,
        preferred_element_type=jnp.float32,
    )
    return (numerator, jnp.sum(weights, axis=4))


def shards(
    tokens,
    norm_gain,
    w_query,
    w_key,
    w_value,
    w_out,
    prompt_keys,
    prompt_values,
    cache_keys,
    cache_values,
    cache_length,
    request_group,
    ancestors,
    accepted,
):
    requests = cache_length.shape[0]
    tree_size = ancestors.shape[1]
    head_dim = prompt_keys.shape[3]
    key_heads = prompt_keys.shape[2]
    query_heads = w_query.shape[1] // head_dim
    group_size = query_heads // key_heads
    slice_rows = prompt_keys.shape[1]
    factor = head_dim ** (-0.5)
    rows_local = tokens.shape[0]
    wide = tokens.astype(jnp.float32)
    normed = (
        wide
        * lax.rsqrt(jnp.mean(wide * wide, axis=1, keepdims=True) + EPS)
        * norm_gain.astype(jnp.float32)
    ).astype(jnp.bfloat16)
    queries = jnp.dot(normed, w_query, preferred_element_type=jnp.float32).reshape(
        rows_local, query_heads, head_dim
    )
    new_keys = jnp.dot(normed, w_key, preferred_element_type=jnp.float32).reshape(
        rows_local, key_heads, head_dim
    )
    new_values = (
        jnp.dot(normed, w_value, preferred_element_type=jnp.float32)
        .astype(jnp.bfloat16)
        .reshape(requests, tree_size, key_heads, head_dim)
    )
    depth = jnp.sum(ancestors, axis=2) - 1
    positions = (PROMPT + cache_length[:, None] + depth).reshape(rows_local)
    queries = rotate_pairs(queries, positions).astype(jnp.bfloat16)
    new_keys = (
        rotate_pairs(new_keys, positions)
        .astype(jnp.bfloat16)
        .reshape(requests, tree_size, key_heads, head_dim)
    )
    grouped = queries.reshape(requests, tree_size, key_heads, group_size, head_dim)
    everyone = lax.all_gather(
        queries.reshape(rows_local, query_heads * head_dim), "tok", axis=0, tiled=True
    )
    all_grouped = everyone.reshape(
        request_group.shape[0], tree_size, key_heads, group_size, head_dim
    )
    chosen_keys = jnp.take(prompt_keys, request_group, axis=0)
    chosen_values = jnp.take(prompt_values, request_group, axis=0)
    outputs, totals = slice_attention(all_grouped, chosen_keys, chosen_values, slice_rows, factor)
    arrived_outputs, arrived_totals = (
        lax.all_to_all(outputs, "tok", split_axis=0, concat_axis=4, tiled=True),
        lax.all_to_all(
            totals.astype(jnp.bfloat16), "tok", split_axis=0, concat_axis=4, tiled=True
        ).astype(totals.dtype),
    )
    prompt_part = jnp.sum(arrived_totals[..., None] * arrived_outputs.astype(jnp.float32), axis=4)
    prompt_total = jnp.sum(arrived_totals, axis=4)
    cache_part, cache_total = cache_block(grouped, cache_keys, cache_values, cache_length, factor)
    tree_scores = (
        jnp.einsum("ntkgd,nmkd->ntkgm", grouped, new_keys, preferred_element_type=jnp.float32)
        * factor
    )
    tree_weights = jnp.where(ancestors[:, :, None, None, :] > 0, jnp.exp(tree_scores), 0.0)
    tree_part = jnp.einsum(
        "ntkgm,nmkd->ntkgd",
        tree_weights.astype(jnp.bfloat16),
        new_values,
        preferred_element_type=jnp.float32,
    )
    denominator = prompt_total + cache_total + jnp.sum(tree_weights, axis=4)
    merged = (prompt_part + cache_part + tree_part) / denominator[..., None]
    attended = merged.astype(jnp.bfloat16).reshape(rows_local, query_heads * head_dim)
    projected = jnp.dot(attended, w_out, preferred_element_type=jnp.float32)
    attention_out = lax.psum_scatter(
        projected.astype(jnp.bfloat16), "mdl", scatter_dimension=1, tiled=True
    )
    columns = attention_out.shape[1]
    column_start = lax.axis_index("mdl") * columns
    residual = lax.dynamic_slice_in_dim(tokens, column_start, columns, 1).astype(
        jnp.float32
    ) + attention_out.astype(jnp.float32)
    rows_index = (
        jnp.arange(requests, dtype=jnp.int32)[:, None] * tree_size + jnp.maximum(accepted, 0)
    ).reshape(requests * accepted.shape[1])
    picked = jnp.take(residual, rows_index, axis=0).reshape(requests, accepted.shape[1], columns)
    compact_rows = jnp.where(accepted[:, :, None] >= 0, picked, 0.0).astype(jnp.bfloat16)
    return (attention_out, compact_rows)


def solution(mesh):
    placed = (
        P("tok", None),
        P(),
        P(None, "mdl"),
        P(None, "mdl"),
        P(None, "mdl"),
        P("mdl", None),
        P(None, "tok", "mdl", None),
        P(None, "tok", "mdl", None),
        P("tok", None, "mdl", None),
        P("tok", None, "mdl", None),
        P("tok"),
        P(),
        P("tok", None, None),
        P("tok", None),
    )
    return jax.shard_map(
        shards,
        mesh=mesh,
        in_specs=placed,
        out_specs=(P("tok", "mdl"), P("tok", None, "mdl")),
        check_vma=False,
    )
```

profile of v0, /device:TPU:0, one launch (start us, length us, event | category | flops | bytes accessed | tf_op | source)
XLA Modules:
  0.0 367.7 jit_solution(15969678895602327398)
XLA Ops:
  8.1 2.3 fusion.18
  12.7 7.9 %fusion.53 = f32[256,1024]{0,1:T(8,128)S(1)} fusion(bf16[5120,1024]{1,0:T(8,128)(2,1)} %param.18, bf16[256,5120]{1,0:T(8,128)(2,1)} %param.16, f32[5120]{0:T(1024)S(1)} %convert_element_type.100, f32[256]{0:T(256)S(1)} %add_rsqrt_fusion), kind=kOutput, calls=%fused_computation.90 | convolution fusion | flops 2689597440 | bytes 14177280 | tf_op jit(solution)/shard_map/reshape | solution.py:96
  21.7 36.4 %gather_fusion.2 = bf16[64,512,2,128]{3,2,1,0:T(2,128)(2,1)} fusion(bf16[6,512,2,128]{3,2,1,0:T(2,128)(2,1)} %param.23, s32[1024]{0:T(1024)S(1)} %pad_clamp_fusion.1), kind=kCustom, calls=%fused_computation.1.clone | custom fusion | bytes 33554688 | tf_op jit(solution)/shard_map/jit(_take)/gather | solution.py:123
  58.1 36.4 %gather_fusion.1 = bf16[64,512,2,128]{3,2,1,0:T(2,128)(2,1)} fusion(bf16[6,512,2,128]{3,2,1,0:T(2,128)(2,1)} %param.22, s32[1024]{0:T(1024)S(1)} %pad_clamp_fusion.1), kind=kCustom, calls=%fused_computation.clone | custom fusion | bytes 33554688 | tf_op jit(solution)/shard_map/jit(_take)/gather | solution.py:122
  94.5 34.1 %fusion.8 = (bf16[64,512,2,128,1]{3,2,1,0,4:T(2,128)(2,1)}, bf16[64,512,2,128,1]{3,2,1,0,4:T(2,128)(2,1)}) fusion(bf16[64,512,2,128]{3,2,1,0:T(2,128)(2,1)} %gather_fusion.2, pred[64]{0:T(512)(128)(4,1)S(1)} %compare_and_fusion.1, bf16[64,512,2,128]{3,2,1,0:T(2,128)(2,1)} %gather_fusion.1), kind=kLoop, calls=%fused_computation.18 | loop fusion | flops 16777216 | bytes 67108928 | tf_op jit(solution)/shard_map/jit(_take)/select_n | solution.py:123
  128.6 6.4 %copy.66 = bf16[2048,1024]{1,0:T(8,128)(2,1)} copy(bf16[2048,1024]{0,1:T(8,128)(2,1)} %all-gather.2.cloned.1.call-done) | data formatting | bytes 8388608 | tf_op jit(solution)/shard_map/all_gather | solution.py:116
  135.0 7.7 %reshape.235 = bf16[64,32,2,4,128]{4,3,2,1,0:T(4,128)(2,1)} reshape(bf16[2048,1024]{1,0:T(8,128)(2,1)} %copy.66) | data formatting | bytes 8388608 | tf_op jit(solution)/shard_map/reshape | solution.py:119
  142.7 22.5 %bitcast_reduce_fusion = (f32[64,32,2,4]{1,3,2,0:T(4,128)S(1)}, f32[64,2,512,32,4]{2,3,4,1,0:T(8,128)}) fusion(bf16[64,32,2,4,128]{4,3,2,1,0:T(4,128)(2,1)} %reshape.235, bf16[64,512,2,128,1]{3,2,1,0,4:T(2,128)(2,1)} %get-tuple-element.15), kind=kOutput, calls=%fused_computation.4 | convolution fusion | flops 2164244480 | bytes 54591488 | tf_op jit(solution)/shard_map/ntkgd,nsckd->ntkgsc/dot_general | solution.py:33
  166.0 1.7 reshape.282
  167.7 7.4 %all-to-all-start = ((bf16[8,2,1024]{2,1,0:T(2,128)(2,1)}), bf16[8,2,1024]{2,1,0:T(2,128)(2,1)}, u32[]{:S(2)}, u32[]{:S(2)}) async-start(bf16[8,2,1024]{2,1,0:T(2,128)(2,1)} %reshape.282), calls=%async_computation | async-start | bytes 65536 | tf_op jit(solution)/shard_map/all_to_all | solution.py:127
  175.0 19.8 %fusion.22 = bf16[64,32,2,4,1,128]{5,1,3,2,4,0:T(8,128)(2,1)} fusion(f32[64,32,2,4]{1,3,2,0:T(4,128)S(1)} %get-tuple-element.16, f32[64,2,512,32,4]{2,3,4,1,0:T(8,128)} %get-tuple-element.17, bf16[64,512,2,128,1]{3,2,1,0,4:T(2,128)(2,1)} %get-tuple-element.14), kind=kOutput, calls=%fused_computation.37 | convolution fusion | flops 2168455168 | bytes 54591488 | tf_op jit(solution)/shard_map/ntkgsc,nsckd->ntkgsd/dot_general | solution.py:38
  194.9 6.1 %all-to-all-start.1 = ((bf16[64,32,2,4,1,128]{5,1,3,2,4,0:T(8,128)(2,1)}), bf16[64,32,2,4,1,128]{5,1,3,2,4,0:T(8,128)(2,1)}, u32[]{:S(2)}, u32[]{:S(2)}) async-start(bf16[64,32,2,4,1,128]{5,1,3,2,4,0:T(8,128)(2,1)} %fusion.22), calls=%async_computation.1 | async-start | bytes 8388608 | tf_op jit(solution)/shard_map/all_to_all | solution.py:126
  204.7 3.1 fusion.50
  208.1 4.1 %convolution_convert_fusion.1 = bf16[256,256]{1,0:T(8,128)(2,1)} fusion(bf16[5120,256]{1,0:T(8,128)(2,1)} %param.20, bf16[256,5120]{1,0:T(8,128)(2,1)} %param.16, f32[5120]{0:T(1024)} %copy-done.3, f32[256]{0:T(256)S(1)} %add_rsqrt_fusion), kind=kOutput, calls=%fused_computation.49 | convolution fusion | flops 676397056 | bytes 5395456 | tf_op jit(solution)/shard_map/dot_general | solution.py:103
  213.3 3.1 fusion.56
  216.4 12.0 %bitcast_reduce_fusion.1 = (f32[8,32,2,4]{1,3,2,0:T(4,128)S(1)}, f32[8,2,32,4,2048]{4,2,3,1,0:T(8,128)}) fusion(pred[8,2048]{1,0:T(8,128)(4,1)S(1)} %iota_compare_fusion, bf16[8,2048,2,128,1]{3,2,1,0,4:T(2,128)(2,1)} %bitcast.123, bf16[8,32,2,4,64]{4,1,0,3,2:T(8,128)(2,1)} %bitcast.112, bf16[8,32,2,4,64]{4,1,0,3,2:T(8,128)(2,1)} %bitcast.114), kind=kOutput, calls=%fused_computation.10 | convolution fusion | flops 1087371264 | bytes 25714688 | tf_op jit(solution)/shard_map/ntkgd,nckd->ntkgc/dot_general | solution.py:50
  229.4 64.3 %all-to-all-done.1 = bf16[64,32,2,4,1,128]{5,1,3,2,4,0:T(8,128)(2,1)} async-done(((bf16[64,32,2,4,1,128]{5,1,3,2,4,0:T(8,128)(2,1)}), bf16[64,32,2,4,1,128]{5,1,3,2,4,0:T(8,128)(2,1)}, u32[]{:S(2)}, u32[]{:S(2)}) %all-to-all-start.1) | async-done | bytes 4194336 | tf_op jit(solution)/shard_map/all_to_all | solution.py:126
  293.7 5.4 %fusion.10 = f32[8,32,2,4,128]{4,1,3,2,0:T(8,128)} fusion(bf16[8,8,32,2,4,1,128]{6,2,4,3,1,0,5:T(8,128)(2,1)} %bitcast.37, f32[8,32,2,4,8]{1,3,2,0,4:T(4,128)S(1)} %bitcast.108), kind=kLoop, calls=%fused_computation.21 | loop fusion | flops 6029312 | bytes 5308416 | tf_op jit(solution)/shard_map/reduce_sum | solution.py:131
  299.2 12.9 %fusion.36 = f32[8,32,2,4,128]{4,1,3,2,0:T(8,128)} fusion(f32[8,32,2,4,128]{4,1,3,2,0:T(8,128)} %fusion.10, bf16[8,2048,2,128,1]{3,2,1,0,4:T(2,128)(2,1)} %bitcast.124, f32[8,2,32,4,2048]{4,2,3,1,0:T(8,128)} %get-tuple-element.21, pred[8,2048]{1,0:T(8,128)(4,1)S(1)} %iota_compare_fusion), kind=kOutput, calls=%fused_computation.48 | convolution fusion | flops 1086586880 | bytes 27279360 | tf_op jit(solution)/shard_map/ntkgc,nckd->ntkgd/dot_general | solution.py:56
  312.1 1.9 fusion.35
  314.3 1.2 reshape.239
  315.4 8.6 %convolution_convert_fusion = bf16[256,5120]{1,0:T(8,128)(2,1)} fusion(bf16[256,1024]{1,0:T(8,128)(2,1)} %reshape.239, bf16[1024,5120]{1,0:T(8,128)(2,1)} %param.21), kind=kOutput, calls=%fused_computation.32 | convolution fusion | flops 2685665280 | bytes 13631488 | tf_op jit(solution)/shard_map/dot_general | solution.py:148
  324.2 33.7 %reduce-scatter.2.cloned.1.call-done = bf16[256,1280]{1,0:T(8,128)(2,1)} async-done(((bf16[256,5120]{1,0:T(8,128)(2,1)}), bf16[256,1280]{1,0:T(8,128)(2,1)}) %reduce-scatter.2.cloned.1.call-update) | async-done | bytes 655376 | tf_op jit(solution)/shard_map/reduce_scatter | solution.py:149
  357.9 1.4 convert_add_fusion
  (58 shorter events, 12.9 us)
Async XLA Ops:
  7.2 197.5 %copy-start = (bf16[5120,256]{1,0:T(8,128)(2,1)S(1)}, bf16[5120,256]{1,0:T(8,128)(2,1)}, u32[]{:S(2)}) copy-start(bf16[5120,256]{1,0:T(8,128)(2,1)} %param.19) | copy-start | bytes 7864324
  7.2 121.4 %all-gather.2.cloned.1.call-start = ((), (), s32[]{:S(2)}) async-start(), calls=%async_computation.3 | async-start | bytes 4718592 | tf_op jit(solution)/shard_map/all_gather | solution.py:116
  8.1 12.6 %copy-start.3 = (f32[5120]{0:T(1024)}, f32[5120]{0:T(1024)S(1)}, u32[]{:S(2)}) copy-start(f32[5120]{0:T(1024)S(1)} %convert_element_type.100) | copy-start | bytes 61444
  12.7 9.0 %copy-start.6 = (s32[64]{0:T(128)S(1)}, s32[64]{0:T(128)}, u32[]{:S(2)}) copy-start(s32[64]{0:T(128)} %param.27) | copy-start | bytes 772
  167.7 27.2 %all-to-all-start = ((bf16[8,2,1024]{2,1,0:T(2,128)(2,1)}), bf16[8,2,1024]{2,1,0:T(2,128)(2,1)}, u32[]{:S(2)}, u32[]{:S(2)}) async-start(bf16[8,2,1024]{2,1,0:T(2,128)(2,1)} %reshape.282), calls=%async_computation | async-start | bytes 65536 | tf_op jit(solution)/shard_map/all_to_all | solution.py:127
  194.9 9.0 %copy-start.1 = (s32[8,32,32]{2,1,0:T(8,128)S(1)}, s32[8,32,32]{2,1,0:T(8,128)}, u32[]{:S(2)}) copy-start(s32[8,32,32]{2,1,0:T(8,128)} %param.28) | copy-start | bytes 98308
  194.9 98.8 %all-to-all-start.1 = ((bf16[64,32,2,4,1,128]{5,1,3,2,4,0:T(8,128)(2,1)}), bf16[64,32,2,4,1,128]{5,1,3,2,4,0:T(8,128)(2,1)}, u32[]{:S(2)}, u32[]{:S(2)}) async-start(bf16[64,32,2,4,1,128]{5,1,3,2,4,0:T(8,128)(2,1)} %fusion.22), calls=%async_computation.1 | async-start | bytes 8388608 | tf_op jit(solution)/shard_map/all_to_all | solution.py:126
  201.0 156.9 %reduce-scatter.2.cloned.1.call-start = ((), (), s32[]{:S(2)}) async-start(), calls=%async_computation.4 | async-start | bytes 3276800 | tf_op jit(solution)/shard_map/reduce_scatter | solution.py:149
  204.7 8.5 %copy-start.2 = (f32[256,64]{1,0:T(8,128)S(1)}, f32[256,64]{1,0:T(8,128)}, u32[]{:S(2)}) copy-start(f32[256,64]{1,0:T(8,128)} %copy.79) | copy-start | bytes 196612
  207.8 8.5 %copy-start.5 = (s32[8]{0:T(128)S(1)}, s32[8]{0:T(128)}, u32[]{:S(2)}) copy-start(s32[8]{0:T(128)} %param.26) | copy-start | bytes 100
  315.4 8.6 %copy-start.4 = (s32[8,8]{1,0:T(8,128)S(1)}, s32[8,8]{1,0:T(8,128)}, u32[]{:S(2)}) copy-start(s32[8,8]{1,0:T(8,128)} %param.29) | copy-start | bytes 772
Sparse Core Ops, SparseCore 0:
  21.8 77.7 all-gather.1
  324.1 33.7 reduce-scatter.1
where the time goes:
time: 369 us; the launch traced here: 368 us
  waiting for transfers between devices  98.1 us (27%)
  local copies, waits for them, and re-layouts  96.6 us (26%)
  matrix products  96 us (26%)
  other arithmetic  49.2 us (13%)
  between operations  14.3 us (4%)
  starting transfers between devices  13.6 us (4%)
    all_to_all x1, waiting for transfers between devices, shards(): lax.all_to_all(outputs, 'tok', split_axis=0, concat_axis=4, tiled=True)  64.3 us
    gather x1, local copies, waits for them, and re-layouts, shards(): chosen_values = jnp.take(prompt_values, request_group, axis=0)  36.4 us
    gather x1, local copies, waits for them, and re-layouts, shards(): chosen_keys = jnp.take(prompt_keys, request_group, axis=0)  36.4 us
    select_n x1, other arithmetic, shards(): chosen_values = jnp.take(prompt_values, request_group, axis=0)  34.1 us
    reduce_scatter x1, waiting for transfers between devices, shards(): lax.psum_scatter(projected.astype(jnp.bfloat16), 'mdl', scatter_dimension...  33.7 us
    dot_general x1, matrix products, slice_attention(): jnp.einsum('ntkgd,nsckd->ntkgsc', grouped, keys_split, preferred_element_...  22.5 us
    dot_general x1, matrix products, slice_attention(): jnp.einsum('ntkgsc,nsckd->ntkgsd', weights.astype(jnp.bfloat16), values_s...  19.8 us
    dot_general x1, matrix products, cache_block(): jnp.einsum('ntkgc,nckd->ntkgd', weights.astype(jnp.bfloat16), value_block...  12.9 us
  transfers between devices with their start and end apart: 4, of which 2 were waited for; matrix products, arithmetic and copies ran while one was open for 42% of the time, Pallas kernels for 0%

commit v1 on v0

v1 whole, which is shorter than its diff:
```python
import functools
import math

import jax
import jax.numpy as jnp
from jax import lax
from jax.experimental import pallas as pl
from jax.experimental.pallas import tpu as pltpu
from jax.sharding import PartitionSpec as P

PROMPT = 4096
THETA = 100000000.0
EPS = 1e-05
PAD = 16
NEG = -1e30
CONTRACT_LAST = (((1,), (1,)), ((), ()))


def rotate_pairs(vectors, positions):
    middle = vectors.shape[-1] // 2
    exponent = jnp.arange(middle, dtype=jnp.float32) * (2.0 / vectors.shape[-1])
    inverse = jnp.power(jnp.float32(THETA), -exponent)
    angles = positions.astype(jnp.float32)[:, None] * inverse[None, :]
    cosine = jnp.cos(angles)[:, None, :]
    sine_part = jnp.sin(angles)[:, None, :]
    leading = vectors[..., :middle]
    trailing = vectors[..., middle:]
    return jnp.concatenate(
        [leading * cosine - trailing * sine_part, trailing * cosine + leading * sine_part], axis=-1
    )


def stack_heads(block, head_dim):
    count = block.shape[1] // head_dim
    return jnp.concatenate(
        [block[:, j * head_dim : (j + 1) * head_dim] for j in range(count)], axis=0
    )


def own_kernel(
    key_heads, chunk, scale, length_ref, q_ref, k_ref, v_ref, tk_ref, tv_ref, mask_ref,
    part_ref, total_ref,
):
    n = pl.program_id(0)
    tree, width = q_ref.shape
    head_dim = k_ref.shape[2]
    query = stack_heads(q_ref[...], head_dim)
    rows = query.shape[0]
    per = rows // key_heads
    live = length_ref[n] * key_heads

    scores = lax.dot_general(query, tk_ref[0], CONTRACT_LAST, preferred_element_type=jnp.float32)
    weights = jnp.exp2(jnp.where(mask_ref[0] > 0, scores * scale, NEG))
    total0 = jnp.sum(weights, axis=1, keepdims=True)
    part0 = jnp.dot(weights.astype(jnp.bfloat16), tv_ref[0], preferred_element_type=jnp.float32)
    row_head = lax.broadcasted_iota(jnp.int32, (rows, chunk), 0) // per
    column = lax.broadcasted_iota(jnp.int32, (rows, chunk), 1)
    own_head = (column % key_heads) == row_head

    def step(i, carry):
        part, total = carry
        start = pl.multiple_of(i * chunk, chunk)
        keys = k_ref[0, pl.ds(start, chunk), :]
        values = v_ref[0, pl.ds(start, chunk), :]
        scores = lax.dot_general(query, keys, CONTRACT_LAST, preferred_element_type=jnp.float32)
        valid = jnp.logical_and(own_head, column < live - start)
        weights = jnp.exp2(jnp.where(valid, scores * scale, NEG))
        total = total + jnp.sum(weights, axis=1, keepdims=True)
        part = part + jnp.dot(
            weights.astype(jnp.bfloat16), values, preferred_element_type=jnp.float32
        )
        return part, total

    part, total = lax.fori_loop(0, (live + chunk - 1) // chunk, step, (part0, total0))
    wide_total = jnp.broadcast_to(total, part.shape)
    for j in range(rows // tree):
        cols = slice(j * head_dim, (j + 1) * head_dim)
        part_ref[:, cols] = part[j * tree : (j + 1) * tree]
        total_ref[:, cols] = wide_total[j * tree : (j + 1) * tree]


def own_attention(queries, cache_keys, cache_values, lengths, tree_keys, tree_values, mask, scale):
    requests, slots, key_heads, head_dim = cache_keys.shape
    rows_local, width = queries.shape
    tree = rows_local // requests
    keys = cache_keys.reshape(requests, slots * key_heads, head_dim)
    values = cache_values.reshape(requests, slots * key_heads, head_dim)
    chunk = 512 * key_heads
    kernel = functools.partial(own_kernel, key_heads, chunk, scale)
    whole = lambda a: pl.BlockSpec((1,) + a.shape[1:], lambda n, _: (n, 0, 0))
    rows_spec = pl.BlockSpec((tree, width), lambda n, _: (n, 0))
    return pl.pallas_call(
        kernel,
        grid_spec=pltpu.PrefetchScalarGridSpec(
            num_scalar_prefetch=1,
            grid=(requests,),
            in_specs=[
                rows_spec, whole(keys), whole(values), whole(tree_keys), whole(tree_values),
                whole(mask),
            ],
            out_specs=[rows_spec, rows_spec],
        ),
        out_shape=[jax.ShapeDtypeStruct((rows_local, width), jnp.float32)] * 2,
        compiler_params=pltpu.CompilerParams(vmem_limit_bytes=40 * 1024 * 1024),
        cost_estimate=pl.CostEstimate(
            flops=8 * rows_local * width * slots * key_heads,
            bytes_accessed=4 * keys.size,
            transcendentals=rows_local * width * slots // 64,
        ),
        name="own_attention",
    )(lengths, queries, keys, values, tree_keys, tree_values, mask)


def prompt_kernel(requests, scale, group_ref, q_ref, *refs):
    key_refs, value_refs, out_ref = refs[0:2], refs[2:4], refs[4]
    step = pl.program_id(0)
    rows, width = q_ref.shape[1:]
    tree = rows // requests
    head_dim = key_refs[0].shape[2]
    heads = width // head_dim
    lanes = heads * tree
    tile_row = lax.broadcasted_iota(jnp.int32, (PAD, lanes), 0)
    totals = jnp.zeros((PAD, lanes), jnp.float32)
    for n in range(requests):
        group = group_ref[step * requests + n]
        query = stack_heads(q_ref[0, n * tree : (n + 1) * tree, :], head_dim)
        part = jnp.zeros((lanes, head_dim), jnp.float32)
        total = jnp.zeros((lanes, 1), jnp.float32)
        for key_ref, value_ref in zip(key_refs, value_refs):
            scores = lax.dot_general(
                query, key_ref[group], CONTRACT_LAST, preferred_element_type=jnp.float32
            )
            weights = jnp.exp2(scores * scale)
            total = total + jnp.sum(weights, axis=1, keepdims=True)
            part = part + jnp.dot(
                weights.astype(jnp.bfloat16), value_ref[group], preferred_element_type=jnp.float32
            )
        turned = jnp.transpose(jnp.broadcast_to(total, (lanes, 128)))[:PAD]
        totals = jnp.where(tile_row == n, turned, totals)
        for j in range(heads):
            out_ref[0, n * tree : (n + 1) * tree, j * head_dim : (j + 1) * head_dim] = part[
                j * tree : (j + 1) * tree
            ].astype(jnp.bfloat16)
    out_ref[0, rows:, :] = jnp.concatenate(
        [totals, jnp.zeros((PAD, width - lanes), jnp.float32)], axis=1
    ).astype(jnp.bfloat16)


def prompt_attention(queries, head, key_heads, groups, keys_pair, values_pair, requests, scale):
    blocks, rows, full = queries.shape
    width = full // key_heads
    whole = lambda a: pl.BlockSpec(a.shape, lambda j, _: (0, 0, 0))
    positions = keys_pair[0].shape[1] * 2
    return pl.pallas_call(
        functools.partial(prompt_kernel, requests, scale),
        grid_spec=pltpu.PrefetchScalarGridSpec(
            num_scalar_prefetch=1,
            grid=(blocks,),
            in_specs=[pl.BlockSpec((1, rows, width), lambda j, _: (j, 0, head))]
            + [whole(a) for a in (*keys_pair, *values_pair)],
            out_specs=pl.BlockSpec((1, rows + PAD, width), lambda j, _: (j, 0, 0)),
        ),
        out_shape=jax.ShapeDtypeStruct((blocks, rows + PAD, width), jnp.bfloat16),
        compiler_params=pltpu.CompilerParams(vmem_limit_bytes=40 * 1024 * 1024),
        cost_estimate=pl.CostEstimate(
            flops=8 * blocks * rows * width * positions,
            bytes_accessed=4 * keys_pair[0].size * 2,
            transcendentals=blocks * rows * width * positions // 128,
        ),
        name="prompt_attention",
    )(groups, queries, *keys_pair, *values_pair)


def add_rounded(left, right):
    return (left.astype(jnp.float32) + right.astype(jnp.float32)).astype(jnp.bfloat16)


def shards(
    n_tok,
    n_mdl,
    tokens,
    norm_gain,
    w_query,
    w_key,
    w_value,
    w_out,
    prompt_keys,
    prompt_values,
    cache_keys,
    cache_values,
    cache_length,
    request_group,
    ancestors,
    accepted,
):
    requests = cache_length.shape[0]
    tree_size = ancestors.shape[1]
    head_dim = prompt_keys.shape[3]
    key_heads = prompt_keys.shape[2]
    query_heads = w_query.shape[1] // head_dim
    group_size = query_heads // key_heads
    scale = head_dim ** (-0.5) * math.log2(math.e)
    rows_local = tokens.shape[0]
    line = n_tok // 2
    swap = [(i, i ^ 1) for i in range(n_tok)]
    tok = lax.axis_index("tok")

    near_keys, near_values, far_keys, far_values = [], [], [], []
    for h in range(key_heads):
        near_keys.append(prompt_keys[:, :, h, :])
        near_values.append(prompt_values[:, :, h, :])
        far_keys.append(lax.ppermute(near_keys[h], "tok", swap))
        far_values.append(lax.ppermute(near_values[h], "tok", swap))

    wide = tokens.astype(jnp.float32)
    normed = (
        wide
        * lax.rsqrt(jnp.mean(wide * wide, axis=1, keepdims=True) + EPS)
        * norm_gain.astype(jnp.float32)
    ).astype(jnp.bfloat16)
    depth = jnp.sum(ancestors, axis=2) - 1
    positions = (PROMPT + cache_length[:, None] + depth).reshape(rows_local)
    queries = jnp.dot(normed, w_query, preferred_element_type=jnp.float32).reshape(
        rows_local, query_heads, head_dim
    )
    queries = (
        rotate_pairs(queries, positions)
        .astype(jnp.bfloat16)
        .reshape(rows_local, query_heads * head_dim)
    )

    def right(value, first, last):
        pairs = [
            (2 * i + y, 2 * (i + 1) + y)
            for i in range(line - 1)
            if first <= i <= last
            for y in range(2)
        ]
        return lax.ppermute(value, "tok", pairs)

    def left(value, first, last):
        pairs = [
            (2 * i + y, 2 * (i - 1) + y)
            for i in range(1, line)
            if first <= i <= last
            for y in range(2)
        ]
        return lax.ppermute(value, "tok", pairs)

    from_left, from_right = [], []
    going_right = going_left = queries
    for s in range(1, line):
        going_right = right(going_right, s - 1, line)
        going_left = left(going_left, 0, line - s)
        from_left.append(going_right)
        from_right.append(going_left)
    place = tok // 2
    blocks = [queries]
    for j in range(1, line):
        blocks.append(jnp.where(place + j < line, from_right[j - 1], from_left[line - j - 1]))
    all_queries = jnp.stack(blocks)
    offsets = jnp.arange(line, dtype=jnp.int32)
    owners = ((place + offsets) % line) * 2 + tok % 2
    groups = jnp.take(request_group.reshape(n_tok, requests), owners, axis=0).reshape(
        line * requests
    )

    new_keys = jnp.dot(normed, w_key, preferred_element_type=jnp.float32).reshape(
        rows_local, key_heads, head_dim
    )
    new_keys = (
        rotate_pairs(new_keys, positions)
        .astype(jnp.bfloat16)
        .reshape(requests, tree_size * key_heads, head_dim)
    )
    new_values = (
        jnp.dot(normed, w_value, preferred_element_type=jnp.float32)
        .astype(jnp.bfloat16)
        .reshape(requests, tree_size * key_heads, head_dim)
    )
    same = jnp.eye(key_heads, dtype=jnp.int32)
    mask = jnp.broadcast_to(
        ancestors[:, None, None, :, :, None] * same[None, :, None, None, None, :],
        (requests, key_heads, group_size, tree_size, tree_size, key_heads),
    ).reshape(requests, query_heads * tree_size, tree_size * key_heads)
    own_part, own_total = own_attention(
        queries, cache_keys, cache_values, cache_length, new_keys, new_values, mask, scale
    )

    merged_heads = []
    width = group_size * head_dim
    for h in range(key_heads):
        messages = prompt_attention(
            all_queries,
            h,
            key_heads,
            groups,
            (near_keys[h], far_keys[h]),
            (near_values[h], far_values[h]),
            requests,
            scale,
        )
        to_right, to_left = messages[line - 1], messages[1 % line]
        for s in range(1, line):
            to_right = right(to_right, 0, s - 1)
            to_left = left(to_left, line - s, line)
            if s < line - 1:
                to_right = add_rounded(messages[line - 1 - s], to_right)
                to_left = add_rounded(messages[s + 1], to_left)
        summed = (
            messages[0].astype(jnp.float32)
            + to_right.astype(jnp.float32)
            + to_left.astype(jnp.float32)
        )
        totals = (
            summed[rows_local : rows_local + requests, : group_size * tree_size]
            .reshape(requests, group_size, tree_size)
            .transpose(0, 2, 1)
            .reshape(rows_local, group_size)
        )
        totals = jnp.broadcast_to(
            totals[:, :, None], (rows_local, group_size, head_dim)
        ).reshape(rows_local, width)
        cols = slice(h * width, (h + 1) * width)
        merged_heads.append(
            (
                (summed[:rows_local] + own_part[:, cols]) / (totals + own_total[:, cols])
            ).astype(jnp.bfloat16)
        )
    attended = jnp.concatenate(merged_heads, axis=1)

    me = lax.axis_index("mdl")
    columns = w_out.shape[1] // n_mdl
    column_start = me * columns
    if n_mdl == 4:
        here, core = me // 2, me % 2

        def project(block):
            piece = lax.dynamic_slice_in_dim(w_out, block * columns, columns, 1)
            return jnp.dot(attended, piece, preferred_element_type=jnp.float32)

        cores = [(i, i ^ 1) for i in range(n_mdl)]
        chips = [(i, i ^ 2) for i in range(n_mdl)]
        far_other = project((1 - here) * 2 + 1 - core).astype(jnp.bfloat16)
        far_other = lax.ppermute(far_other, "mdl", cores)
        far_mine = project((1 - here) * 2 + core)
        far_sum = (far_mine + far_other.astype(jnp.float32)).astype(jnp.bfloat16)
        arrived = lax.ppermute(far_sum, "mdl", chips)
        near_other = project(here * 2 + 1 - core).astype(jnp.bfloat16)
        near_other = lax.ppermute(near_other, "mdl", cores)
        near_mine = project(me)
        attention_out = (
            near_mine + near_other.astype(jnp.float32) + arrived.astype(jnp.float32)
        ).astype(jnp.bfloat16)
    else:
        projected = jnp.dot(attended, w_out, preferred_element_type=jnp.float32)
        attention_out = lax.psum_scatter(
            projected.astype(jnp.bfloat16), "mdl", scatter_dimension=1, tiled=True
        )
    residual = lax.dynamic_slice_in_dim(tokens, column_start, columns, 1).astype(
        jnp.float32
    ) + attention_out.astype(jnp.float32)
    rows_index = (
        jnp.arange(requests, dtype=jnp.int32)[:, None] * tree_size + jnp.maximum(accepted, 0)
    ).reshape(requests * accepted.shape[1])
    picked = jnp.take(residual, rows_index, axis=0).reshape(requests, accepted.shape[1], columns)
    compact_rows = jnp.where(accepted[:, :, None] >= 0, picked, 0.0).astype(jnp.bfloat16)
    return (attention_out, compact_rows)


def solution(mesh):
    placed = (
        P("tok", None),
        P(),
        P(None, "mdl"),
        P(None, "mdl"),
        P(None, "mdl"),
        P("mdl", None),
        P(None, "tok", "mdl", None),
        P(None, "tok", "mdl", None),
        P("tok", None, "mdl", None),
        P("tok", None, "mdl", None),
        P("tok"),
        P(),
        P("tok", None, None),
        P("tok", None),
    )
    return jax.shard_map(
        functools.partial(shards, mesh.shape["tok"], mesh.shape["mdl"]),
        mesh=mesh,
        in_specs=placed,
        out_specs=(P("tok", "mdl"), P("tok", None, "mdl")),
        check_vma=False,
    )
```

time: 369 us -> 209 us (0.57)
  matrix products: 96 us -> 25.3 us
  local copies, waits for them, and re-layouts: 96.6 us -> 31.1 us
  waiting for transfers between devices: 98.1 us -> 40.9 us
  starting transfers between devices: 13.6 us -> 50.1 us
  Pallas kernels: 0 us -> 34.1 us
  other arithmetic: 49.2 us -> 23.5 us
  between operations: 14.3 us -> 1.37 us
    gather x2 -> x1, local copies, waits for them, and re-layouts: 72.7 us -> 0.56 us  [shards(): jnp.take(request_group.reshape(n_tok, requests), owners, axis=0)]
    all_to_all x2 -> x0, waiting for transfers between devices: 64.3 us -> none  [the longest x1 64.3 us: shards(): lax.all_to_all(outputs, 'tok', split_axis=0, concat_axis=4, tiled=True)]
    dot_general x7 -> x5, matrix products: 80.8 us -> 18.1 us  [the longest x4 12.3 us: project(): return jnp.dot(attended, piece, preferred_element_type=jnp.float32)]
    ppermute x0 -> x25, starting transfers between devices: none -> 50.1 us  [the longest x9 32.4 us: right(): return lax.ppermute(value, 'tok', pairs)]
    ppermute x0 -> x25, waiting for transfers between devices: none -> 40.9 us  [the longest x9 19.7 us: left(): return lax.ppermute(value, 'tok', pairs)]
    pallas_call x0 -> x3, Pallas kernels: none -> 34.1 us  [the longest x2 21.8 us: prompt_attention(): pl.pallas_call(functools.partial(prompt_kernel, requests, scale), grid_sp...]
    select_n x2, other arithmetic: 34.1 us -> 0.09 us  [shards(): jnp.take(request_group.reshape(n_tok, requests), owners, axis=0)]
    reduce_scatter x1 -> x0, waiting for transfers between devices: 33.7 us -> none  [shards(): lax.psum_scatter(projected.astype(jnp.bfloat16), 'mdl', scatter_dimension...]
  transfers between devices with their start and end apart: 4 -> 25, of which waited for: 2 -> 5; matrix products, arithmetic and copies ran while one was open for 42% -> 23% of each run, Pallas kernels for 0% -> 17%
where the time goes in v1:
time: 209 us; the launch traced here: 206 us
  starting transfers between devices  50.1 us (24%)
  waiting for transfers between devices  40.9 us (20%)
  Pallas kernels  34.1 us (16%)
  local copies, waits for them, and re-layouts  31.1 us (15%)
  matrix products  25.3 us (12%)
  other arithmetic  23.5 us (11%)
    ppermute x9, starting transfers between devices, right(): return lax.ppermute(value, 'tok', pairs)  32.4 us
    pallas_call x2, Pallas kernels, prompt_attention(): pl.pallas_call(functools.partial(prompt_kernel, requests, scale), grid_sp...  21.8 us
    ppermute x9, waiting for transfers between devices, left(): return lax.ppermute(value, 'tok', pairs)  19.7 us
    unnamed x67, local copies, waits for them, and re-layouts  14.7 us
    ppermute x1, waiting for transfers between devices, shards(): arrived = lax.ppermute(far_sum, 'mdl', chips)  12.6 us
    pallas_call x1, Pallas kernels, own_attention(): pl.pallas_call(kernel, grid_spec=pltpu.PrefetchScalarGridSpec(num_scalar_...  12.4 us
    dot_general x4, matrix products, project(): return jnp.dot(attended, piece, preferred_element_type=jnp.float32)  12.3 us
    ppermute x9, starting transfers between devices, left(): return lax.ppermute(value, 'tok', pairs)  11 us
  transfers between devices with their start and end apart: 25, of which 5 were waited for; matrix products, arithmetic and copies ran while one was open for 23% of the time, Pallas kernels for 17%

profile of v1, /device:TPU:0, one launch (start us, length us, event | category | flops | bytes accessed | tf_op | source)
XLA Modules:
  0.0 206.4 jit_solution(17725851261730150578)
XLA Ops:
  4.0 5.8 %convolution_bitcast_fusion = f32[32,8,8,128]{3,1,2,0:T(8,128)S(1)} fusion(bf16[5120,1024]{1,0:T(8,128)(2,1)} %param.16, bf16[256,5120]{1,0:T(8,128)(2,1)S(1)} %copy-done.14, f32[5120]{0:T(1024)S(1)} %convert_element_type.184, f32[256]{0:T(256)S(1)} %add_rsqrt_fusion), kind=kOutput, calls=%fused_computation.18 | convolution fusion | flops 2689597440 | bytes 14177280 | tf_op jit(solution)/shard_map/dot_general | solution.py:223
  15.3 5.7 %collective-permute-start.1 = (bf16[256,1024]{1,0:T(8,128)(2,1)}, bf16[256,1024]{1,0:T(8,128)(2,1)}, u32[]{:S(2)}, u32[]{:S(2)}) collective-permute-start(bf16[256,1024]{1,0:T(8,128)(2,1)} %bitcast.106.q_ref), channel_id=1, source_target_pairs={{0,8},{4,12},{8,16},{12,20},{16,24},{20,28},{1,9},{5,13},{9,17},{1... | collective-permute-start | bytes 1572872 | tf_op jit(solution)/shard_map/ppermute | solution.py:239
  27.2 3.1 %fusion.47 = (bf16[6,512,1,128]{3,2,1,0:T(2,128)(2,1)}, bf16[6,512,1,128]{3,2,1,0:T(2,128)(2,1)S(1)}) fusion(bf16[6,512,2,128]{3,2,1,0:T(2,128)(2,1)S(1)} %copy-done.11), kind=kLoop, calls=%fused_computation.112 | loop fusion | bytes 3145728 | tf_op jit(solution)/shard_map/slice | solution.py:211
  33.5 3.3 %convolution_convert_fusion = bf16[256,256]{1,0:T(8,128)(2,1)} fusion(bf16[5120,256]{1,0:T(8,128)(2,1)S(1)} %copy-done, bf16[256,5120]{1,0:T(8,128)(2,1)} %param.14, f32[5120]{0:T(1024)} %copy-done.26, f32[256]{0:T(256)S(1)} %add_rsqrt_fusion), kind=kOutput, calls=%fused_computation.22 | convolution fusion | flops 676397056 | bytes 5395456 | tf_op jit(solution)/shard_map/dot_general | solution.py:277
  36.8 4.0 %fusion.44 = f32[256,256]{0,1:T(8,128)S(1)} fusion(bf16[5120,256]{1,0:T(8,128)(2,1)} %param.17, bf16[256,5120]{1,0:T(8,128)(2,1)} %param.14, f32[5120]{0:T(1024)} %copy-done.26, f32[256]{0:T(256)S(1)} %add_rsqrt_fusion), kind=kOutput, calls=%fused_computation.111 | convolution fusion | flops 676331520 | bytes 5526528 | tf_op jit(solution)/shard_map/dot_general | solution.py:268
  49.8 11.0 %collective-permute-done.4 = bf16[256,1024]{1,0:T(8,128)(2,1)} collective-permute-done((bf16[256,1024]{1,0:T(8,128)(2,1)}, bf16[256,1024]{1,0:T(8,128)(2,1)}, u32[]{:S(2)}, u32[]{:S(2)}) %collective-permute-start.4) | collective-permute-done | bytes 524320 | tf_op jit(solution)/shard_map/ppermute | solution.py:248
  65.5 8.7 %collective-permute-done.5 = bf16[256,1024]{1,0:T(8,128)(2,1)S(1)} collective-permute-done((bf16[256,1024]{1,0:T(8,128)(2,1)}, bf16[256,1024]{1,0:T(8,128)(2,1)S(1)}, u32[]{:S(2)}, u32[]{:S(2)}) %collective-permute-start.5) | collective-permute-done | bytes 524320 | tf_op jit(solution)/shard_map/ppermute | solution.py:248
  74.6 11.3 %prompt_attention.3 = bf16[4,272,512]{2,1,0:T(8,128)(2,1)S(1)} custom-call(s32[32]{0:T(128)S(1)} %select_n.125.group_ref, bf16[4,256,1024]{2,1,0:T(8,128)(2,1)S(1)} %pad_maximum_fusion.q_ref, bf16[6,512,128]{2,1,0:T(8,128)(2,1)} %bitcast.103.refs_0_, bf16[6,512,128]{2,1,0:T(8,128)(2,1)} %collective-permute-done.14.refs_1_, ...), custom_call_target="tpu_custom_call" | custom-call | flops 4294967296 | bytes 3145728 | tf_op jit(solution)/shard_map/prompt_attention/pallas_call | solution.py:154
  85.9 2.6 %collective-permute-start.16 = (bf16[272,512]{1,0:T(8,128)(2,1)S(1)}, bf16[272,512]{1,0:T(8,128)(2,1)S(1)}, u32[]{:S(2)}, u32[]{:S(2)}) collective-permute-start(bf16[272,512]{1,0:T(8,128)(2,1)S(1)} %get-tuple-element.28), channel_id=1, source_target_pairs={{0,8},{4,12},{1,9},{5,13},{2,10},{6,14},{3,11},{7,15}} | collective-permute-start | bytes 835592 | tf_op jit(solution)/shard_map/ppermute | solution.py:239
  89.3 6.1 %collective-permute-done.7.refs_3_ = bf16[6,512,128]{2,1,0:T(8,128)(2,1)S(1)} collective-permute-done((bf16[6,512,128]{2,1,0:T(8,128)(2,1)S(1)}, bf16[6,512,128]{2,1,0:T(8,128)(2,1)S(1)}, u32[]{:S(2)}, u32[]{:S(2)}) %collective-permute-start.7) | collective-permute-done | bytes 786464 | tf_op jit(solution)/shard_map/ppermute | solution.py:213
  95.4 10.5 %prompt_attention.2 = bf16[4,272,512]{2,1,0:T(8,128)(2,1)S(1)} custom-call(s32[32]{0:T(128)S(1)} %select_n.125.group_ref, bf16[4,256,1024]{2,1,0:T(8,128)(2,1)S(1)} %pad_maximum_fusion.q_ref, bf16[6,512,128]{2,1,0:T(8,128)(2,1)S(1)} %bitcast.108, bf16[6,512,128]{2,1,0:T(8,128)(2,1)} %collective-permute-done.6.refs_1_, bf16[6,512,128]{2,1,0:T(8,128)(2,1)S(1)} %bitcast.110, ...), custom_call_target="tpu_custom_call" | custom-call | flops 4294967296 | bytes 3145728 | tf_op jit(solution)/shard_map/prompt_attention/pallas_call | solution.py:154
  106.7 4.3 %collective-permute-start.8 = (bf16[272,512]{1,0:T(8,128)(2,1)S(1)}, bf16[272,512]{1,0:T(8,128)(2,1)S(1)}, u32[]{:S(2)}, u32[]{:S(2)}) collective-permute-start(bf16[272,512]{1,0:T(8,128)(2,1)S(1)} %get-tuple-element.22), channel_id=1, source_target_pairs={{0,8},{4,12},{1,9},{5,13},{2,10},{6,14},{3,11},{7,15}} | collective-permute-start | bytes 835592 | tf_op jit(solution)/shard_map/ppermute | solution.py:239
  120.4 5.0 %collective-permute-start.9 = (bf16[272,512]{1,0:T(8,128)(2,1)}, bf16[272,512]{1,0:T(8,128)(2,1)}, u32[]{:S(2)}, u32[]{:S(2)}) collective-permute-start(bf16[272,512]{1,0:T(8,128)(2,1)} %get-tuple-element.20), channel_id=1, source_target_pairs={{0,8},{4,12},{8,16},{12,20},{1,9},{5,13},{9,17},{13,21},{2,10},{6,... | collective-permute-start | bytes 835592 | tf_op jit(solution)/shard_map/ppermute | solution.py:239
  128.2 3.4 %reshape.284 = s32[8,256,64]{1,2,0:T(8,128)} reshape(s32[8,2,4,32,32,2]{3,2,1,5,4,0:T(4,128)} %broadcast_in_dim.68) | data formatting | bytes 1048576 | tf_op jit(solution)/shard_map/reshape | solution.py:285
  135.0 4.6 %collective-permute-start.18 = (bf16[272,512]{1,0:T(8,128)(2,1)}, bf16[272,512]{1,0:T(8,128)(2,1)}, u32[]{:S(2)}, u32[]{:S(2)}) collective-permute-start(bf16[272,512]{1,0:T(8,128)(2,1)} %get-tuple-element.24), channel_id=1, source_target_pairs={{0,8},{4,12},{8,16},{12,20},{16,24},{20,28},{1,9},{5,13},{9,17},{1... | collective-permute-start | bytes 835592 | tf_op jit(solution)/shard_map/ppermute | solution.py:239
  142.9 5.3 %collective-permute-start.10 = (bf16[272,512]{1,0:T(8,128)(2,1)}, bf16[272,512]{1,0:T(8,128)(2,1)}, u32[]{:S(2)}, u32[]{:S(2)}) collective-permute-start(bf16[272,512]{1,0:T(8,128)(2,1)} %get-tuple-element.18), channel_id=1, source_target_pairs={{0,8},{4,12},{8,16},{12,20},{16,24},{20,28},{1,9},{5,13},{9,17},{1... | collective-permute-start | bytes 835592 | tf_op jit(solution)/shard_map/ppermute | solution.py:239
  149.6 3.4 %copy-done.8 = bf16[8,2048,2,128]{3,2,1,0:T(2,128)(2,1)S(1)} copy-done((bf16[8,2048,2,128]{3,2,1,0:T(2,128)(2,1)S(1)}, bf16[8,2048,2,128]{3,2,1,0:T(2,128)(2,1)}, u32[]{:S(2)}) %copy-start.8) | copy-done | bytes 8388632
  153.0 12.4 %own_attention.1 = (f32[256,1024]{1,0:T(8,128)S(1)}, f32[256,1024]{1,0:T(8,128)S(1)}) custom-call(s32[8]{0:T(128)S(1)} %copy-done.9, bf16[256,1024]{1,0:T(8,128)(2,1)} %bitcast.106.q_ref, bf16[8,4096,128]{2,1,0:T(8,128)(2,1)S(1)} %bitcast.111, bf16[8,4096,128]{2,1,0:T(8,128)(2,1)} %bitcast.121, bf16[8,64,128]{2,1,0:T(8,128)(2,1)S(1)} %pad_maximum_fusion.2.tk_ref, ...), custom_call_target="tpu_custom_call" | custom-call | flops 8589934592 | bytes 16777216 | tf_op jit(solution)/shard_map/own_attention/pallas_call | solution.py:92
  175.0 2.6 %fusion.14 = bf16[256,1280]{1,0:T(8,128)(2,1)S(1)} fusion(bf16[1024,5120]{1,0:T(8,128)(2,1)} %param.19, s32[]{:T(128)S(6)} %select_n.137, bf16[256,512]{1,0:T(8,128)(2,1)S(1)} %get-tuple-element.11, bf16[256,512]{1,0:T(8,128)(2,1)S(1)} %get-tuple-element.10), kind=kOutput, calls=%fused_computation.16 | convolution fusion | flops 672464896 | bytes 3801092 | tf_op jit(solution)/shard_map/dot_general | solution.py:340
  177.8 3.6 %fusion.11 = bf16[256,1280]{1,0:T(8,128)(2,1)} fusion(bf16[1024,5120]{1,0:T(8,128)(2,1)} %param.19, s32[]{:T(128)S(6)} %select_n.135, bf16[256,512]{1,0:T(8,128)(2,1)} %copy-done.19, bf16[256,512]{1,0:T(8,128)(2,1)S(1)} %get-tuple-element.10), kind=kOutput, calls=%fused_computation.15 | convolution fusion | flops 672464896 | bytes 3801092 | tf_op jit(solution)/shard_map/dot_general | solution.py:340
  181.8 3.4 %add_convert_fusion.1 = bf16[256,1280]{1,0:T(8,128)(2,1)} fusion(bf16[256,1280]{1,0:T(8,128)(2,1)S(1)} %collective-permute-done.23, bf16[1024,5120]{1,0:T(8,128)(2,1)} %param.19, s32[]{:T(128)S(6)} %select_n.136, bf16[256,512]{1,0:T(8,128)(2,1)S(1)} %copy-done.20, bf16[256,512]{1,0:T(8,128)(2,1)S(1)} %get-tuple-element.10), kind=kOutput, calls=%fused_computation.21 | convolution fusion | flops 673120256 | bytes 4456452 | tf_op jit(solution)/shard_map/dot_general | solution.py:340
  186.9 2.7 %fusion.9 = f32[256,1280]{1,0:T(8,128)S(1)} fusion(bf16[1024,5120]{1,0:T(8,128)(2,1)} %param.19, s32[]{:T(128)S(6)} %select_n.132, bf16[256,512]{1,0:T(8,128)(2,1)S(1)} %copy-done.20, bf16[256,512]{1,0:T(8,128)(2,1)S(1)} %get-tuple-element.10), kind=kOutput, calls=%fused_computation.13 | convolution fusion | flops 672137216 | bytes 4456452 | tf_op jit(solution)/shard_map/dot_general | solution.py:340
  189.6 12.6 %collective-permute-done.24 = bf16[256,1280]{1,0:T(8,128)(2,1)} collective-permute-done((bf16[256,1280]{1,0:T(8,128)(2,1)}, bf16[256,1280]{1,0:T(8,128)(2,1)}, u32[]{:S(2)}, u32[]{:S(2)}) %collective-permute-start.24) | collective-permute-done | bytes 655392 | tf_op jit(solution)/shard_map/ppermute | solution.py:348
  202.2 2.7 %convert_add_fusion = (bf16[256,1280]{1,0:T(8,128)(2,1)S(1)}, bf16[256,1280]{1,0:T(8,128)(2,1)}) fusion(bf16[256,5120]{1,0:T(8,128)(2,1)} %param.14, s32[]{:T(128)S(6)} %select_n.132, bf16[256,1280]{1,0:T(8,128)(2,1)} %collective-permute-done.24, f32[256,1280]{1,0:T(8,128)S(1)} %fusion.9, bf16[256,1280]{1,0:T(8,128)(2,1)} %collective-permute-done.22), kind=kLoop, calls=%fused_computation.19 | loop fusion | flops 2949120 | bytes 4587524 | tf_op jit(solution)/shard_map/add | solution.py:360
  (162 shorter events, 67.2 us)
Async XLA Ops:
  15.3 26.1 %collective-permute-start.1 = (bf16[256,1024]{1,0:T(8,128)(2,1)}, bf16[256,1024]{1,0:T(8,128)(2,1)}, u32[]{:S(2)}, u32[]{:S(2)}) collective-permute-start(bf16[256,1024]{1,0:T(8,128)(2,1)} %bitcast.106.q_ref), channel_id=1, source_target_pairs={{0,8},{4,12},{8,16},{12,20},{16,24},{20,28},{1,9},{5,13},{9,17},{1... | collective-permute-start | bytes 1572872 | tf_op jit(solution)/shard_map/ppermute | solution.py:239
  21.1 22.6 %collective-permute-start = (bf16[256,1024]{1,0:T(8,128)(2,1)}, bf16[256,1024]{1,0:T(8,128)(2,1)}, u32[]{:S(2)}, u32[]{:S(2)}) collective-permute-start(bf16[256,1024]{1,0:T(8,128)(2,1)} %bitcast.106.q_ref), channel_id=1, source_target_pairs={{8,0},{12,4},{16,8},{20,12},{24,16},{28,20},{9,1},{13,5},{17,9},{2... | collective-permute-start | bytes 1572872 | tf_op jit(solution)/shard_map/ppermute | solution.py:248
  25.6 48.9 %collective-permute-start.14 = (bf16[6,512,128]{2,1,0:T(8,128)(2,1)}, bf16[6,512,128]{2,1,0:T(8,128)(2,1)}, u32[]{:S(2)}, u32[]{:S(2)}) collective-permute-start(bf16[6,512,128]{2,1,0:T(8,128)(2,1)} %bitcast.103.refs_0_), channel_id=1, source_target_pairs={{0,4},{4,0},{8,12},{12,8},{16,20},{20,16},{24,28},{28,24},{1,5},{5... | collective-permute-start | bytes 2359304 | tf_op jit(solution)/shard_map/ppermute | solution.py:212
  31.2 43.3 %collective-permute-start.15 = (bf16[6,512,128]{2,1,0:T(8,128)(2,1)}, bf16[6,512,128]{2,1,0:T(8,128)(2,1)}, u32[]{:S(2)}, u32[]{:S(2)}) collective-permute-start(bf16[6,512,128]{2,1,0:T(8,128)(2,1)} %bitcast.102.refs_2_), channel_id=1, source_target_pairs={{0,4},{4,0},{8,12},{12,8},{16,20},{20,16},{24,28},{28,24},{1,5},{5... | collective-permute-start | bytes 2359304 | tf_op jit(solution)/shard_map/ppermute | solution.py:213
  32.0 57.3 %collective-permute-start.6 = (bf16[6,512,128]{2,1,0:T(8,128)(2,1)S(1)}, bf16[6,512,128]{2,1,0:T(8,128)(2,1)}, u32[]{:S(2)}, u32[]{:S(2)}) collective-permute-start(bf16[6,512,128]{2,1,0:T(8,128)(2,1)S(1)} %bitcast.107), channel_id=1, source_target_pairs={{0,4},{4,0},{8,12},{12,8},{16,20},{20,16},{24,28},{28,24},{1,5},{5... | collective-permute-start | bytes 2359304 | tf_op jit(solution)/shard_map/ppermute | solution.py:212
  43.6 17.1 %collective-permute-start.4 = (bf16[256,1024]{1,0:T(8,128)(2,1)}, bf16[256,1024]{1,0:T(8,128)(2,1)}, u32[]{:S(2)}, u32[]{:S(2)}) collective-permute-start(bf16[256,1024]{1,0:T(8,128)(2,1)} %collective-permute-done), channel_id=1, source_target_pairs={{8,0},{12,4},{16,8},{20,12},{9,1},{13,5},{17,9},{21,13},{10,2},{14... | collective-permute-start | bytes 1572872 | tf_op jit(solution)/shard_map/ppermute | solution.py:248
  45.0 18.3 %collective-permute-start.3 = (bf16[256,1024]{1,0:T(8,128)(2,1)}, bf16[256,1024]{1,0:T(8,128)(2,1)}, u32[]{:S(2)}, u32[]{:S(2)}) collective-permute-start(bf16[256,1024]{1,0:T(8,128)(2,1)} %collective-permute-done.2), channel_id=1, source_target_pairs={{16,24},{20,28},{17,25},{21,29},{18,26},{22,30},{19,27},{23,31}} | collective-permute-start | bytes 1572872 | tf_op jit(solution)/shard_map/ppermute | solution.py:239
  60.8 13.4 %collective-permute-start.5 = (bf16[256,1024]{1,0:T(8,128)(2,1)}, bf16[256,1024]{1,0:T(8,128)(2,1)S(1)}, u32[]{:S(2)}, u32[]{:S(2)}) collective-permute-start(bf16[256,1024]{1,0:T(8,128)(2,1)} %collective-permute-done.4), channel_id=1, source_target_pairs={{8,0},{12,4},{9,1},{13,5},{10,2},{14,6},{11,3},{15,7}} | collective-permute-start | bytes 1572872 | tf_op jit(solution)/shard_map/ppermute | solution.py:248
  63.4 32.1 %collective-permute-start.7 = (bf16[6,512,128]{2,1,0:T(8,128)(2,1)S(1)}, bf16[6,512,128]{2,1,0:T(8,128)(2,1)S(1)}, u32[]{:S(2)}, u32[]{:S(2)}) collective-permute-start(bf16[6,512,128]{2,1,0:T(8,128)(2,1)S(1)} %bitcast.109), channel_id=1, source_target_pairs={{0,4},{4,0},{8,12},{12,8},{16,20},{20,16},{24,28},{28,24},{1,5},{5... | collective-permute-start | bytes 2359304 | tf_op jit(solution)/shard_map/ppermute | solution.py:213
  85.9 25.3 %collective-permute-start.16 = (bf16[272,512]{1,0:T(8,128)(2,1)S(1)}, bf16[272,512]{1,0:T(8,128)(2,1)S(1)}, u32[]{:S(2)}, u32[]{:S(2)}) collective-permute-start(bf16[272,512]{1,0:T(8,128)(2,1)S(1)} %get-tuple-element.28), channel_id=1, source_target_pairs={{0,8},{4,12},{1,9},{5,13},{2,10},{6,14},{3,11},{7,15}} | collective-permute-start | bytes 835592 | tf_op jit(solution)/shard_map/ppermute | solution.py:239
  88.5 22.7 %collective-permute-start.19 = (bf16[272,512]{1,0:T(8,128)(2,1)S(1)}, bf16[272,512]{1,0:T(8,128)(2,1)S(1)}, u32[]{:S(2)}, u32[]{:S(2)}) collective-permute-start(bf16[272,512]{1,0:T(8,128)(2,1)S(1)} %get-tuple-element.29), channel_id=1, source_target_pairs={{24,16},{28,20},{25,17},{29,21},{26,18},{30,22},{27,19},{31,23}} | collective-permute-start | bytes 835592 | tf_op jit(solution)/shard_map/ppermute | solution.py:248
  106.0 9.6 %collective-permute-start.11 = (bf16[272,512]{1,0:T(8,128)(2,1)S(1)}, bf16[272,512]{1,0:T(8,128)(2,1)S(1)}, u32[]{:S(2)}, u32[]{:S(2)}) collective-permute-start(bf16[272,512]{1,0:T(8,128)(2,1)S(1)} %get-tuple-element.23), channel_id=1, source_target_pairs={{24,16},{28,20},{25,17},{29,21},{26,18},{30,22},{27,19},{31,23}} | collective-permute-start | bytes 835592 | tf_op jit(solution)/shard_map/ppermute | solution.py:248
  106.7 11.4 %collective-permute-start.8 = (bf16[272,512]{1,0:T(8,128)(2,1)S(1)}, bf16[272,512]{1,0:T(8,128)(2,1)S(1)}, u32[]{:S(2)}, u32[]{:S(2)}) collective-permute-start(bf16[272,512]{1,0:T(8,128)(2,1)S(1)} %get-tuple-element.22), channel_id=1, source_target_pairs={{0,8},{4,12},{1,9},{5,13},{2,10},{6,14},{3,11},{7,15}} | collective-permute-start | bytes 835592 | tf_op jit(solution)/shard_map/ppermute | solution.py:239
  112.2 20.7 %collective-permute-start.17 = (bf16[272,512]{1,0:T(8,128)(2,1)}, bf16[272,512]{1,0:T(8,128)(2,1)}, u32[]{:S(2)}, u32[]{:S(2)}) collective-permute-start(bf16[272,512]{1,0:T(8,128)(2,1)} %get-tuple-element.26), channel_id=1, source_target_pairs={{0,8},{4,12},{8,16},{12,20},{1,9},{5,13},{9,17},{13,21},{2,10},{6,... | collective-permute-start | bytes 835592 | tf_op jit(solution)/shard_map/ppermute | solution.py:239
  114.2 18.8 %collective-permute-start.20 = (bf16[272,512]{1,0:T(8,128)(2,1)}, bf16[272,512]{1,0:T(8,128)(2,1)}, u32[]{:S(2)}, u32[]{:S(2)}) collective-permute-start(bf16[272,512]{1,0:T(8,128)(2,1)} %get-tuple-element.27), channel_id=1, source_target_pairs={{16,8},{20,12},{24,16},{28,20},{17,9},{21,13},{25,17},{29,21},{18,... | collective-permute-start | bytes 835592 | tf_op jit(solution)/shard_map/ppermute | solution.py:248
  119.0 21.8 %collective-permute-start.12 = (bf16[272,512]{1,0:T(8,128)(2,1)}, bf16[272,512]{1,0:T(8,128)(2,1)}, u32[]{:S(2)}, u32[]{:S(2)}) collective-permute-start(bf16[272,512]{1,0:T(8,128)(2,1)} %get-tuple-element.21), channel_id=1, source_target_pairs={{16,8},{20,12},{24,16},{28,20},{17,9},{21,13},{25,17},{29,21},{18,... | collective-permute-start | bytes 835592 | tf_op jit(solution)/shard_map/ppermute | solution.py:248
  120.4 20.5 %collective-permute-start.9 = (bf16[272,512]{1,0:T(8,128)(2,1)}, bf16[272,512]{1,0:T(8,128)(2,1)}, u32[]{:S(2)}, u32[]{:S(2)}) collective-permute-start(bf16[272,512]{1,0:T(8,128)(2,1)} %get-tuple-element.20), channel_id=1, source_target_pairs={{0,8},{4,12},{8,16},{12,20},{1,9},{5,13},{9,17},{13,21},{2,10},{6,... | collective-permute-start | bytes 835592 | tf_op jit(solution)/shard_map/ppermute | solution.py:239
  135.0 32.4 %collective-permute-start.18 = (bf16[272,512]{1,0:T(8,128)(2,1)}, bf16[272,512]{1,0:T(8,128)(2,1)}, u32[]{:S(2)}, u32[]{:S(2)}) collective-permute-start(bf16[272,512]{1,0:T(8,128)(2,1)} %get-tuple-element.24), channel_id=1, source_target_pairs={{0,8},{4,12},{8,16},{12,20},{16,24},{20,28},{1,9},{5,13},{9,17},{1... | collective-permute-start | bytes 835592 | tf_op jit(solution)/shard_map/ppermute | solution.py:239
  139.5 27.9 %collective-permute-start.21 = (bf16[272,512]{1,0:T(8,128)(2,1)}, bf16[272,512]{1,0:T(8,128)(2,1)}, u32[]{:S(2)}, u32[]{:S(2)}) collective-permute-start(bf16[272,512]{1,0:T(8,128)(2,1)} %get-tuple-element.25), channel_id=1, source_target_pairs={{8,0},{12,4},{16,8},{20,12},{24,16},{28,20},{9,1},{13,5},{17,9},{2... | collective-permute-start | bytes 835592 | tf_op jit(solution)/shard_map/ppermute | solution.py:248
  142.9 26.8 %collective-permute-start.10 = (bf16[272,512]{1,0:T(8,128)(2,1)}, bf16[272,512]{1,0:T(8,128)(2,1)}, u32[]{:S(2)}, u32[]{:S(2)}) collective-permute-start(bf16[272,512]{1,0:T(8,128)(2,1)} %get-tuple-element.18), channel_id=1, source_target_pairs={{0,8},{4,12},{8,16},{12,20},{16,24},{20,28},{1,9},{5,13},{9,17},{1... | collective-permute-start | bytes 835592 | tf_op jit(solution)/shard_map/ppermute | solution.py:239
  148.1 21.6 %collective-permute-start.13 = (bf16[272,512]{1,0:T(8,128)(2,1)}, bf16[272,512]{1,0:T(8,128)(2,1)}, u32[]{:S(2)}, u32[]{:S(2)}) collective-permute-start(bf16[272,512]{1,0:T(8,128)(2,1)} %get-tuple-element.19), channel_id=1, source_target_pairs={{8,0},{12,4},{16,8},{20,12},{24,16},{28,20},{9,1},{13,5},{17,9},{2... | collective-permute-start | bytes 835592 | tf_op jit(solution)/shard_map/ppermute | solution.py:248
  177.6 4.1 %collective-permute-start.23 = (bf16[256,1280]{1,0:T(8,128)(2,1)S(1)}, bf16[256,1280]{1,0:T(8,128)(2,1)S(1)}, u32[]{:S(2)}, u32[]{:S(2)}) collective-permute-start(bf16[256,1280]{1,0:T(8,128)(2,1)S(1)} %fusion.14), channel_id=1, source_target_pairs={{0,1},{1,0},{2,3},{3,2},{4,5},{5,4},{6,7},{7,6},{8,9},{9,8},{10,11... | collective-permute-start | bytes 1966088 | tf_op jit(solution)/shard_map/ppermute | solution.py:345
  181.3 8.3 %collective-permute-start.22 = (bf16[256,1280]{1,0:T(8,128)(2,1)}, bf16[256,1280]{1,0:T(8,128)(2,1)}, u32[]{:S(2)}, u32[]{:S(2)}) collective-permute-start(bf16[256,1280]{1,0:T(8,128)(2,1)} %fusion.11), channel_id=1, source_target_pairs={{0,1},{1,0},{2,3},{3,2},{4,5},{5,4},{6,7},{7,6},{8,9},{9,8},{10,11... | collective-permute-start | bytes 1966088 | tf_op jit(solution)/shard_map/ppermute | solution.py:350
  185.2 17.0 %collective-permute-start.24 = (bf16[256,1280]{1,0:T(8,128)(2,1)}, bf16[256,1280]{1,0:T(8,128)(2,1)}, u32[]{:S(2)}, u32[]{:S(2)}) collective-permute-start(bf16[256,1280]{1,0:T(8,128)(2,1)} %add_convert_fusion.1), channel_id=1, source_target_pairs={{0,2},{1,3},{2,0},{3,1},{4,6},{5,7},{6,4},{7,5},{8,10},{9,11},{10,... | collective-permute-start | bytes 1966088 | tf_op jit(solution)/shard_map/ppermute | solution.py:348
  (30 other events, 237.5 us)

commit v2 on v1

--- a/solution.py
+++ b/solution.py
@@ -49,10 +49,16 @@
     per = rows // key_heads
     live = length_ref[n] * key_heads
 
-    scores = lax.dot_general(query, tk_ref[0], CONTRACT_LAST, preferred_element_type=jnp.float32)
-    weights = jnp.exp2(jnp.where(mask_ref[0] > 0, scores * scale, NEG))
+    tree_keys = stack_heads(tk_ref[...], head_dim)
+    tree_values = stack_heads(tv_ref[...], head_dim)
+    lineage = jnp.concatenate([mask_ref[0]] * (rows // tree), axis=0)
+    tree_row = lax.broadcasted_iota(jnp.int32, lineage.shape, 0) // per
+    tree_column = lax.broadcasted_iota(jnp.int32, lineage.shape, 1) // tree
+    scores = lax.dot_general(query, tree_keys, CONTRACT_LAST, preferred_element_type=jnp.float32)
+    allowed = jnp.logical_and(lineage > 0, tree_row == tree_column)
+    weights = jnp.exp2(jnp.where(allowed, scores * scale, NEG))
     total0 = jnp.sum(weights, axis=1, keepdims=True)
-    part0 = jnp.dot(weights.astype(jnp.bfloat16), tv_ref[0], preferred_element_type=jnp.float32)
+    part0 = jnp.dot(weights.astype(jnp.bfloat16), tree_values, preferred_element_type=jnp.float32)
     row_head = lax.broadcasted_iota(jnp.int32, (rows, chunk), 0) // per
     column = lax.broadcasted_iota(jnp.int32, (rows, chunk), 1)
     own_head = (column % key_heads) == row_head
@@ -89,14 +95,14 @@
     kernel = functools.partial(own_kernel, key_heads, chunk, scale)
     whole = lambda a: pl.BlockSpec((1,) + a.shape[1:], lambda n, _: (n, 0, 0))
     rows_spec = pl.BlockSpec((tree, width), lambda n, _: (n, 0))
+    tree_spec = pl.BlockSpec((tree, tree_keys.shape[1]), lambda n, _: (n, 0))
     return pl.pallas_call(
         kernel,
         grid_spec=pltpu.PrefetchScalarGridSpec(
             num_scalar_prefetch=1,
             grid=(requests,),
             in_specs=[
-                rows_spec, whole(keys), whole(values), whole(tree_keys), whole(tree_values),
-                whole(mask),
+                rows_spec, whole(keys), whole(values), tree_spec, tree_spec, whole(mask),
             ],
             out_specs=[rows_spec, rows_spec],
         ),
@@ -112,11 +118,12 @@
 
 
 def prompt_kernel(requests, scale, group_ref, q_ref, *refs):
-    key_refs, value_refs, out_ref = refs[0:2], refs[2:4], refs[4]
+    pair, out_ref = refs[:2], refs[2]
+    group_count = pair[0].shape[0] // 2
     step = pl.program_id(0)
     rows, width = q_ref.shape[1:]
     tree = rows // requests
-    head_dim = key_refs[0].shape[2]
+    head_dim = pair[0].shape[2]
     heads = width // head_dim
     lanes = heads * tree
     tile_row = lax.broadcasted_iota(jnp.int32, (PAD, lanes), 0)
@@ -126,14 +133,16 @@
         query = stack_heads(q_ref[0, n * tree : (n + 1) * tree, :], head_dim)
         part = jnp.zeros((lanes, head_dim), jnp.float32)
         total = jnp.zeros((lanes, 1), jnp.float32)
-        for key_ref, value_ref in zip(key_refs, value_refs):
+        for prompt_ref in pair:
             scores = lax.dot_general(
-                query, key_ref[group], CONTRACT_LAST, preferred_element_type=jnp.float32
+                query, prompt_ref[group], CONTRACT_LAST, preferred_element_type=jnp.float32
             )
             weights = jnp.exp2(scores * scale)
             total = total + jnp.sum(weights, axis=1, keepdims=True)
             part = part + jnp.dot(
-                weights.astype(jnp.bfloat16), value_ref[group], preferred_element_type=jnp.float32
+                weights.astype(jnp.bfloat16),
+                prompt_ref[group_count + group],
+                preferred_element_type=jnp.float32,
             )
         turned = jnp.transpose(jnp.broadcast_to(total, (lanes, 128)))[:PAD]
         totals = jnp.where(tile_row == n, turned, totals)
@@ -146,29 +155,29 @@
     ).astype(jnp.bfloat16)
 
 
-def prompt_attention(queries, head, key_heads, groups, keys_pair, values_pair, requests, scale):
+def prompt_attention(queries, head, key_heads, groups, pair, requests, scale):
     blocks, rows, full = queries.shape
     width = full // key_heads
     whole = lambda a: pl.BlockSpec(a.shape, lambda j, _: (0, 0, 0))
-    positions = keys_pair[0].shape[1] * 2
+    positions = pair[0].shape[1] * 2
     return pl.pallas_call(
         functools.partial(prompt_kernel, requests, scale),
         grid_spec=pltpu.PrefetchScalarGridSpec(
             num_scalar_prefetch=1,
             grid=(blocks,),
             in_specs=[pl.BlockSpec((1, rows, width), lambda j, _: (j, 0, head))]
-            + [whole(a) for a in (*keys_pair, *values_pair)],
+            + [whole(a) for a in pair],
             out_specs=pl.BlockSpec((1, rows + PAD, width), lambda j, _: (j, 0, 0)),
         ),
         out_shape=jax.ShapeDtypeStruct((blocks, rows + PAD, width), jnp.bfloat16),
         compiler_params=pltpu.CompilerParams(vmem_limit_bytes=40 * 1024 * 1024),
         cost_estimate=pl.CostEstimate(
             flops=8 * blocks * rows * width * positions,
-            bytes_accessed=4 * keys_pair[0].size * 2,
+            bytes_accessed=4 * pair[0].size,
             transcendentals=blocks * rows * width * positions // 128,
         ),
         name="prompt_attention",
-    )(groups, queries, *keys_pair, *values_pair)
+    )(groups, queries, *pair)
 
 
 def add_rounded(left, right):
@@ -205,12 +214,12 @@
     swap = [(i, i ^ 1) for i in range(n_tok)]
     tok = lax.axis_index("tok")
 
-    near_keys, near_values, far_keys, far_values = [], [], [], []
-    for h in range(key_heads):
-        near_keys.append(prompt_keys[:, :, h, :])
-        near_values.append(prompt_values[:, :, h, :])
-        far_keys.append(lax.ppermute(near_keys[h], "tok", swap))
-        far_values.append(lax.ppermute(near_values[h], "tok", swap))
+    near = [
+        jnp.concatenate([prompt_keys[:, :, h, :], prompt_values[:, :, h, :]], axis=0)
+        for h in range(key_heads)
+    ]
+    tokens, near = lax.optimization_barrier((tokens, near))
+    far = [lax.ppermute(piece, "tok", swap) for piece in near]
 
     wide = tokens.astype(jnp.float32)
     normed = (
@@ -271,21 +280,15 @@
     new_keys = (
         rotate_pairs(new_keys, positions)
         .astype(jnp.bfloat16)
-        .reshape(requests, tree_size * key_heads, head_dim)
-    )
-    new_values = (
-        jnp.dot(normed, w_value, preferred_element_type=jnp.float32)
-        .astype(jnp.bfloat16)
-        .reshape(requests, tree_size * key_heads, head_dim)
-    )
-    same = jnp.eye(key_heads, dtype=jnp.int32)
-    mask = jnp.broadcast_to(
-        ancestors[:, None, None, :, :, None] * same[None, :, None, None, None, :],
-        (requests, key_heads, group_size, tree_size, tree_size, key_heads),
-    ).reshape(requests, query_heads * tree_size, tree_size * key_heads)
+        .reshape(rows_local, key_heads * head_dim)
+    )
+    new_values = jnp.dot(normed, w_value, preferred_element_type=jnp.float32).astype(jnp.bfloat16)
+    mask = jnp.concatenate([ancestors] * key_heads, axis=2)
     own_part, own_total = own_attention(
         queries, cache_keys, cache_values, cache_length, new_keys, new_values, mask, scale
     )
+
+    all_queries, own_part, own_total = lax.optimization_barrier((all_queries, own_part, own_total))
 
     merged_heads = []
     width = group_size * head_dim
@@ -295,8 +298,7 @@
             h,
             key_heads,
             groups,
-            (near_keys[h], far_keys[h]),
-            (near_values[h], far_values[h]),
+            (near[h], far[h]),
             requests,
             scale,
         )
@@ -327,7 +329,6 @@
                 (summed[:rows_local] + own_part[:, cols]) / (totals + own_total[:, cols])
             ).astype(jnp.bfloat16)
         )
-    attended = jnp.concatenate(merged_heads, axis=1)
 
     me = lax.axis_index("mdl")
     columns = w_out.shape[1] // n_mdl
@@ -337,7 +338,14 @@
 
         def project(block):
             piece = lax.dynamic_slice_in_dim(w_out, block * columns, columns, 1)
-            return jnp.dot(attended, piece, preferred_element_type=jnp.float32)
+            return sum(
+                jnp.dot(
+                    part,
+                    piece[h * width : (h + 1) * width],
+                    preferred_element_type=jnp.float32,
+                )
+                for h, part in enumerate(merged_heads)
+            )
 
         cores = [(i, i ^ 1) for i in range(n_mdl)]
         chips = [(i, i ^ 2) for i in range(n_mdl)]
@@ -353,6 +361,7 @@
             near_mine + near_other.astype(jnp.float32) + arrived.astype(jnp.float32)
         ).astype(jnp.bfloat16)
     else:
+        attended = jnp.concatenate(merged_heads, axis=1)
         projected = jnp.dot(attended, w_out, preferred_element_type=jnp.float32)
         attention_out = lax.psum_scatter(
             projected.astype(jnp.bfloat16), "mdl", scatter_dimension=1, tiled=True

time: 209 us -> 194 us (0.928)
  local copies, waits for them, and re-layouts: 31.1 us -> 22.2 us
  starting transfers between devices: 50.1 us -> 41.3 us
  waiting for transfers between devices: 40.9 us -> 47.6 us
  other arithmetic: 23.5 us -> 21.1 us
    ppermute x9, waiting for transfers between devices: 19.7 us -> 34 us  [left(): return lax.ppermute(value, 'tok', pairs)]
    ppermute x9, starting transfers between devices: 32.4 us -> 26.3 us  [right(): return lax.ppermute(value, 'tok', pairs)]
    ppermute x4 -> x2, waiting for transfers between devices: 6.1 us -> 0.01 us  [shards(): far = [lax.ppermute(piece, 'tok', swap) for piece in near]]
    reshape x3 -> x0, local copies, waits for them, and re-layouts: 5.72 us -> none  [the longest x2 4.77 us: shards(): mask = jnp.broadcast_to(ancestors[:, None, None, :, :, None] * same[None,...]
    unnamed x67 -> x59, local copies, waits for them, and re-layouts: 14.7 us -> 10.1 us
    concatenate x0 -> x3, other arithmetic: none -> 2.69 us  [the longest x2 2.59 us: shards(): jnp.concatenate([prompt_keys[:, :, h, :], prompt_values[:, :, h, :]], axi...]
    dot_general x1, matrix products: 3.97 us -> 1.36 us  [shards(): jnp.dot(normed, w_key, preferred_element_type=jnp.float32)]
    ppermute x4 -> x2, starting transfers between devices: 4.62 us -> 2.09 us  [shards(): far = [lax.ppermute(piece, 'tok', swap) for piece in near]]
  transfers between devices with their start and end apart: 25 -> 23, of which waited for: 5 -> 6; matrix products, arithmetic and copies ran while one was open for 23% -> 16% of each run, Pallas kernels for 17% -> 17%
where the time goes in v2:
time: 194 us; the launch traced here: 192 us
  waiting for transfers between devices  47.6 us (25%)
  starting transfers between devices  41.3 us (21%)
  Pallas kernels  33.4 us (17%)
  matrix products  25.1 us (13%)
  local copies, waits for them, and re-layouts  22.2 us (11%)
  other arithmetic  21.1 us (11%)
    ppermute x9, waiting for transfers between devices, left(): return lax.ppermute(value, 'tok', pairs)  34 us
    ppermute x9, starting transfers between devices, right(): return lax.ppermute(value, 'tok', pairs)  26.3 us
    pallas_call x2, Pallas kernels, prompt_attention(): pl.pallas_call(functools.partial(prompt_kernel, requests, scale), grid_sp...  22.6 us
    dot_general x8, matrix products, project(): jnp.dot(part, piece[h * width:(h + 1) * width], preferred_element_type=jn...  14.6 us
    ppermute x1, waiting for transfers between devices, shards(): arrived = lax.ppermute(far_sum, 'mdl', chips)  11.3 us
    pallas_call x1, Pallas kernels, own_attention(): pl.pallas_call(kernel, grid_spec=pltpu.PrefetchScalarGridSpec(num_scalar_...  10.8 us
    ppermute x9, starting transfers between devices, left(): return lax.ppermute(value, 'tok', pairs)  10.7 us
    unnamed x59, local copies, waits for them, and re-layouts  10.1 us
  transfers between devices with their start and end apart: 23, of which 6 were waited for; matrix products, arithmetic and copies ran while one was open for 16% of the time, Pallas kernels for 17%

profile of v2, /device:TPU:0, one launch (start us, length us, event | category | flops | bytes accessed | tf_op | source)
XLA Modules:
  0.0 192.0 jit_solution(9560742134070647623)
XLA Ops:
  0.7 4.5 %fusion.45 = (bf16[6,512,1,128]{3,2,1,0:T(2,128)(2,1)S(1)}, bf16[6,512,1,128]{3,2,1,0:T(2,128)(2,1)S(1)}) fusion(bf16[6,512,2,128]{3,2,1,0:T(2,128)(2,1)} %param.20), kind=kLoop, calls=%fused_computation.121 | loop fusion | bytes 3145728 | tf_op jit(solution)/shard_map/slice | solution.py:218
  5.2 2.2 %fusion.46 = (bf16[6,512,1,128]{3,2,1,0:T(2,128)(2,1)S(1)}, bf16[6,512,1,128]{3,2,1,0:T(2,128)(2,1)S(1)}) fusion(bf16[6,512,2,128]{3,2,1,0:T(2,128)(2,1)S(1)} %copy-done.6), kind=kLoop, calls=%fused_computation.122 | loop fusion | bytes 3145728 | tf_op jit(solution)/shard_map/slice | solution.py:218
  12.8 6.5 %convolution_bitcast_fusion = f32[32,8,8,128]{3,1,2,0:T(8,128)S(1)} fusion(bf16[5120,1024]{1,0:T(8,128)(2,1)} %param.16, bf16[256,5120]{1,0:T(8,128)(2,1)} %param.14, f32[5120]{0:T(1024)S(1)} %convert_element_type.180, f32[256]{0:T(256)S(1)} %add_rsqrt_fusion), kind=kOutput, calls=%fused_computation.16 | convolution fusion | flops 2689597440 | bytes 14177280 | tf_op jit(solution)/shard_map/dot_general | solution.py:232
  21.8 5.8 %collective-permute-start.1 = (bf16[256,1024]{1,0:T(8,128)(2,1)}, bf16[256,1024]{1,0:T(8,128)(2,1)}, u32[]{:S(2)}, u32[]{:S(2)}) collective-permute-start(bf16[256,1024]{1,0:T(8,128)(2,1)} %bitcast.109.q_ref), channel_id=1, source_target_pairs={{0,8},{4,12},{8,16},{12,20},{16,24},{20,28},{1,9},{5,13},{9,17},{1... | collective-permute-start | bytes 1572872 | tf_op jit(solution)/shard_map/ppermute | solution.py:248
  35.1 2.6 %convolution_convert_fusion.tv_ref = bf16[256,256]{1,0:T(8,128)(2,1)S(1)} fusion(bf16[5120,256]{1,0:T(8,128)(2,1)} %param.18, bf16[256,5120]{1,0:T(8,128)(2,1)S(1)} %copy-done.11, f32[5120]{0:T(1024)S(1)} %copy-done.19, f32[256]{0:T(256)S(1)} %add_rsqrt_fusion), kind=kOutput, calls=%fused_computation.32 | convolution fusion | flops 676397056 | bytes 5395456 | tf_op jit(solution)/shard_map/dot_general | solution.py:285
  38.9 3.4 %copy-done.4 = bf16[8,2048,2,128]{3,2,1,0:T(2,128)(2,1)S(1)} copy-done((bf16[8,2048,2,128]{3,2,1,0:T(2,128)(2,1)S(1)}, bf16[8,2048,2,128]{3,2,1,0:T(2,128)(2,1)}, u32[]{:S(2)}) %copy-start.4) | copy-done | bytes 8388632
  42.3 10.8 %own_attention.1 = (f32[256,1024]{1,0:T(8,128)S(1)}, f32[256,1024]{1,0:T(8,128)S(1)}) custom-call(s32[8]{0:T(128)S(1)} %copy-done.5, bf16[256,1024]{1,0:T(8,128)(2,1)} %bitcast.109.q_ref, bf16[8,4096,128]{2,1,0:T(8,128)(2,1)S(1)} %bitcast.112, bf16[8,4096,128]{2,1,0:T(8,128)(2,1)} %bitcast.121, bf16[256,256]{1,0:T(8,128)(2,1)S(1)} %bitcast.111, ...), custom_call_target="tpu_custom_call" | custom-call | flops 8589934592 | bytes 16777216 | tf_op jit(solution)/shard_map/own_attention/pallas_call | solution.py:99
  58.0 19.0 %collective-permute-done.4 = bf16[256,1024]{1,0:T(8,128)(2,1)} collective-permute-done((bf16[256,1024]{1,0:T(8,128)(2,1)}, bf16[256,1024]{1,0:T(8,128)(2,1)}, u32[]{:S(2)}, u32[]{:S(2)}) %collective-permute-start.4) | collective-permute-done | bytes 524320 | tf_op jit(solution)/shard_map/ppermute | solution.py:257
  80.7 10.2 %collective-permute-done.5 = bf16[256,1024]{1,0:T(8,128)(2,1)S(1)} collective-permute-done((bf16[256,1024]{1,0:T(8,128)(2,1)}, bf16[256,1024]{1,0:T(8,128)(2,1)S(1)}, u32[]{:S(2)}, u32[]{:S(2)}) %collective-permute-start.5) | collective-permute-done | bytes 524320 | tf_op jit(solution)/shard_map/ppermute | solution.py:257
  91.2 11.3 %prompt_attention.2 = bf16[4,272,512]{2,1,0:T(8,128)(2,1)S(1)} custom-call(s32[32]{0:T(128)S(1)} %select_n.125.group_ref, bf16[4,256,1024]{2,1,0:T(8,128)(2,1)S(1)} %pad_maximum_fusion.q_ref, bf16[12,512,128]{2,1,0:T(8,128)(2,1)} %pad_maximum_fusion.1.refs_0_, bf16[12,512,128]{2,1,0:T(8,128)(2,1)} %collective-permute-done.6.refs_1_), custom_call_target="tpu_custom_call" | custom-call | flops 4294967296 | bytes 3145728 | tf_op jit(solution)/shard_map/prompt_attention/pallas_call | solution.py:163
  103.3 2.6 %collective-permute-start.7 = (bf16[272,512]{1,0:T(8,128)(2,1)S(1)}, bf16[272,512]{1,0:T(8,128)(2,1)S(1)}, u32[]{:S(2)}, u32[]{:S(2)}) collective-permute-start(bf16[272,512]{1,0:T(8,128)(2,1)S(1)} %get-tuple-element.40), channel_id=1, source_target_pairs={{0,8},{4,12},{1,9},{5,13},{2,10},{6,14},{3,11},{7,15}} | collective-permute-start | bytes 835592 | tf_op jit(solution)/shard_map/ppermute | solution.py:248
  105.9 11.3 %prompt_attention.3 = bf16[4,272,512]{2,1,0:T(8,128)(2,1)S(1)} custom-call(s32[32]{0:T(128)S(1)} %select_n.125.group_ref, bf16[4,256,1024]{2,1,0:T(8,128)(2,1)S(1)} %pad_maximum_fusion.q_ref, bf16[12,512,128]{2,1,0:T(8,128)(2,1)} %pad_maximum_fusion.2.refs_0_, bf16[12,512,128]{2,1,0:T(8,128)(2,1)} %collective-permute-done.13.refs_1_), custom_call_target="tpu_custom_call" | custom-call | flops 4294967296 | bytes 3145728 | tf_op jit(solution)/shard_map/prompt_attention/pallas_call | solution.py:163
  121.5 2.0 %collective-permute-start.8 = (bf16[272,512]{1,0:T(8,128)(2,1)S(1)}, bf16[272,512]{1,0:T(8,128)(2,1)}, u32[]{:S(2)}, u32[]{:S(2)}) collective-permute-start(bf16[272,512]{1,0:T(8,128)(2,1)S(1)} %get-tuple-element.38), channel_id=1, source_target_pairs={{0,8},{4,12},{8,16},{12,20},{1,9},{5,13},{9,17},{13,21},{2,10},{6,... | collective-permute-start | bytes 835592 | tf_op jit(solution)/shard_map/ppermute | solution.py:248
  126.2 5.1 %collective-permute-start.15 = (bf16[272,512]{1,0:T(8,128)(2,1)}, bf16[272,512]{1,0:T(8,128)(2,1)}, u32[]{:S(2)}, u32[]{:S(2)}) collective-permute-start(bf16[272,512]{1,0:T(8,128)(2,1)} %get-tuple-element.32), channel_id=1, source_target_pairs={{0,8},{4,12},{8,16},{12,20},{1,9},{5,13},{9,17},{13,21},{2,10},{6,... | collective-permute-start | bytes 835592 | tf_op jit(solution)/shard_map/ppermute | solution.py:248
  134.7 1.9 add_convert_fusion.5
  137.8 5.3 %collective-permute-start.9 = (bf16[272,512]{1,0:T(8,128)(2,1)S(1)}, bf16[272,512]{1,0:T(8,128)(2,1)}, u32[]{:S(2)}, u32[]{:S(2)}) collective-permute-start(bf16[272,512]{1,0:T(8,128)(2,1)S(1)} %get-tuple-element.36), channel_id=1, source_target_pairs={{0,8},{4,12},{8,16},{12,20},{16,24},{20,28},{1,9},{5,13},{9,17},{1... | collective-permute-start | bytes 835592 | tf_op jit(solution)/shard_map/ppermute | solution.py:248
  143.1 2.0 %add_convert_fusion.3 = (bf16[272,512]{1,0:T(8,128)(2,1)}, bf16[272,512]{1,0:T(8,128)(2,1)}) fusion(bf16[272,512]{1,0:T(8,128)(2,1)} %collective-permute-done.15, bf16[4,272,512]{2,1,0:T(8,128)(2,1)S(1)} %prompt_attention.3, bf16[272,512]{1,0:T(8,128)(2,1)} %collective-permute-done.18), kind=kLoop, calls=%fused_computation.53 | loop fusion | flops 1114112 | bytes 1671168 | tf_op jit(solution)/shard_map/convert_element_type | solution.py:184
  145.1 2.0 %collective-permute-start.16 = (bf16[272,512]{1,0:T(8,128)(2,1)}, bf16[272,512]{1,0:T(8,128)(2,1)}, u32[]{:S(2)}, u32[]{:S(2)}) collective-permute-start(bf16[272,512]{1,0:T(8,128)(2,1)} %get-tuple-element.30), channel_id=1, source_target_pairs={{0,8},{4,12},{8,16},{12,20},{16,24},{20,28},{1,9},{5,13},{9,17},{1... | collective-permute-start | bytes 835592 | tf_op jit(solution)/shard_map/ppermute | solution.py:248
  151.1 4.7 %collective-permute-done.19 = bf16[272,512]{1,0:T(8,128)(2,1)} collective-permute-done((bf16[272,512]{1,0:T(8,128)(2,1)}, bf16[272,512]{1,0:T(8,128)(2,1)}, u32[]{:S(2)}, u32[]{:S(2)}) %collective-permute-start.19) | collective-permute-done | bytes 278560 | tf_op jit(solution)/shard_map/ppermute | solution.py:257
  161.5 1.8 fusion.4
  165.2 1.8 fusion.3
  169.5 1.9 add_convert_fusion.1
  176.7 11.3 %collective-permute-done.22 = bf16[256,1280]{1,0:T(8,128)(2,1)S(1)} collective-permute-done((bf16[256,1280]{1,0:T(8,128)(2,1)S(1)}, bf16[256,1280]{1,0:T(8,128)(2,1)S(1)}, u32[]{:S(2)}, u32[]{:S(2)}) %collective-permute-start.22) | collective-permute-done | bytes 655392 | tf_op jit(solution)/shard_map/ppermute | solution.py:356
  188.0 2.4 %convert_add_fusion = (bf16[256,1280]{1,0:T(8,128)(2,1)S(1)}, bf16[256,1280]{1,0:T(8,128)(2,1)}) fusion(bf16[256,5120]{1,0:T(8,128)(2,1)} %param.14, s32[]{:T(128)S(6)} %select_n.132, bf16[256,1280]{1,0:T(8,128)(2,1)S(1)} %collective-permute-done.22, f32[256,1280]{1,0:T(8,128)S(1)} %convolution_add_fusion.3, bf16[256,1280]{1,0:T(8,128)(2,1)S(1)} %collective-permute-done.20), kind=kLoop, calls=%fused_computation.29 | loop fusion | flops 2949120 | bytes 4587524 | tf_op jit(solution)/shard_map/add | solution.py:369
  (153 shorter events, 58.2 us)
Async XLA Ops:
  0.6 30.4 %copy-start = (bf16[5120,256]{1,0:T(8,128)(2,1)S(1)}, bf16[5120,256]{1,0:T(8,128)(2,1)}, u32[]{:S(2)}) copy-start(bf16[5120,256]{1,0:T(8,128)(2,1)} %param.17) | copy-start | bytes 7864324
  21.8 16.4 %collective-permute-start.1 = (bf16[256,1024]{1,0:T(8,128)(2,1)}, bf16[256,1024]{1,0:T(8,128)(2,1)}, u32[]{:S(2)}, u32[]{:S(2)}) collective-permute-start(bf16[256,1024]{1,0:T(8,128)(2,1)} %bitcast.109.q_ref), channel_id=1, source_target_pairs={{0,8},{4,12},{8,16},{12,20},{16,24},{20,28},{1,9},{5,13},{9,17},{1... | collective-permute-start | bytes 1572872 | tf_op jit(solution)/shard_map/ppermute | solution.py:248
  27.6 26.5 %collective-permute-start = (bf16[256,1024]{1,0:T(8,128)(2,1)}, bf16[256,1024]{1,0:T(8,128)(2,1)}, u32[]{:S(2)}, u32[]{:S(2)}) collective-permute-start(bf16[256,1024]{1,0:T(8,128)(2,1)} %bitcast.109.q_ref), channel_id=1, source_target_pairs={{8,0},{12,4},{16,8},{20,12},{24,16},{28,20},{9,1},{13,5},{17,9},{2... | collective-permute-start | bytes 1572872 | tf_op jit(solution)/shard_map/ppermute | solution.py:257
  28.9 62.3 %collective-permute-start.6 = (bf16[12,512,128]{2,1,0:T(8,128)(2,1)}, bf16[12,512,128]{2,1,0:T(8,128)(2,1)}, u32[]{:S(2)}, u32[]{:S(2)}) collective-permute-start(bf16[12,512,128]{2,1,0:T(8,128)(2,1)} %pad_maximum_fusion.1.refs_0_), channel_id=1, source_target_pairs={{0,4},{4,0},{8,12},{12,8},{16,20},{20,16},{24,28},{28,24},{1,5},{5... | collective-permute-start | bytes 4718600 | tf_op jit(solution)/shard_map/ppermute | solution.py:222
  30.5 75.4 %collective-permute-start.13 = (bf16[12,512,128]{2,1,0:T(8,128)(2,1)}, bf16[12,512,128]{2,1,0:T(8,128)(2,1)}, u32[]{:S(2)}, u32[]{:S(2)}) collective-permute-start(bf16[12,512,128]{2,1,0:T(8,128)(2,1)} %pad_maximum_fusion.2.refs_0_), channel_id=1, source_target_pairs={{0,4},{4,0},{8,12},{12,8},{16,20},{20,16},{24,28},{28,24},{1,5},{5... | collective-permute-start | bytes 4718600 | tf_op jit(solution)/shard_map/ppermute | solution.py:222
  38.2 17.2 %collective-permute-start.2 = (bf16[256,1024]{1,0:T(8,128)(2,1)}, bf16[256,1024]{1,0:T(8,128)(2,1)S(1)}, u32[]{:S(2)}, u32[]{:S(2)}) collective-permute-start(bf16[256,1024]{1,0:T(8,128)(2,1)} %collective-permute-done.1), channel_id=1, source_target_pairs={{8,16},{12,20},{16,24},{20,28},{9,17},{13,21},{17,25},{21,29},{10,... | collective-permute-start | bytes 1572872 | tf_op jit(solution)/shard_map/ppermute | solution.py:248
  54.1 22.9 %collective-permute-start.4 = (bf16[256,1024]{1,0:T(8,128)(2,1)}, bf16[256,1024]{1,0:T(8,128)(2,1)}, u32[]{:S(2)}, u32[]{:S(2)}) collective-permute-start(bf16[256,1024]{1,0:T(8,128)(2,1)} %collective-permute-done), channel_id=1, source_target_pairs={{8,0},{12,4},{16,8},{20,12},{9,1},{13,5},{17,9},{21,13},{10,2},{14... | collective-permute-start | bytes 1572872 | tf_op jit(solution)/shard_map/ppermute | solution.py:257
  55.4 24.1 %collective-permute-start.3 = (bf16[256,1024]{1,0:T(8,128)(2,1)S(1)}, bf16[256,1024]{1,0:T(8,128)(2,1)}, u32[]{:S(2)}, u32[]{:S(2)}) collective-permute-start(bf16[256,1024]{1,0:T(8,128)(2,1)S(1)} %collective-permute-done.2), channel_id=1, source_target_pairs={{16,24},{20,28},{17,25},{21,29},{18,26},{22,30},{19,27},{23,31}} | collective-permute-start | bytes 1572872 | tf_op jit(solution)/shard_map/ppermute | solution.py:248
  77.0 13.9 %collective-permute-start.5 = (bf16[256,1024]{1,0:T(8,128)(2,1)}, bf16[256,1024]{1,0:T(8,128)(2,1)S(1)}, u32[]{:S(2)}, u32[]{:S(2)}) collective-permute-start(bf16[256,1024]{1,0:T(8,128)(2,1)} %collective-permute-done.4), channel_id=1, source_target_pairs={{8,0},{12,4},{9,1},{13,5},{10,2},{14,6},{11,3},{15,7}} | collective-permute-start | bytes 1572872 | tf_op jit(solution)/shard_map/ppermute | solution.py:257
  102.6 16.7 %collective-permute-start.10 = (bf16[272,512]{1,0:T(8,128)(2,1)S(1)}, bf16[272,512]{1,0:T(8,128)(2,1)S(1)}, u32[]{:S(2)}, u32[]{:S(2)}) collective-permute-start(bf16[272,512]{1,0:T(8,128)(2,1)S(1)} %get-tuple-element.41), channel_id=1, source_target_pairs={{24,16},{28,20},{25,17},{29,21},{26,18},{30,22},{27,19},{31,23}} | collective-permute-start | bytes 835592 | tf_op jit(solution)/shard_map/ppermute | solution.py:257
  103.3 16.0 %collective-permute-start.7 = (bf16[272,512]{1,0:T(8,128)(2,1)S(1)}, bf16[272,512]{1,0:T(8,128)(2,1)S(1)}, u32[]{:S(2)}, u32[]{:S(2)}) collective-permute-start(bf16[272,512]{1,0:T(8,128)(2,1)S(1)} %get-tuple-element.40), channel_id=1, source_target_pairs={{0,8},{4,12},{1,9},{5,13},{2,10},{6,14},{3,11},{7,15}} | collective-permute-start | bytes 835592 | tf_op jit(solution)/shard_map/ppermute | solution.py:248
  117.3 8.0 %collective-permute-start.14 = (bf16[272,512]{1,0:T(8,128)(2,1)S(1)}, bf16[272,512]{1,0:T(8,128)(2,1)S(1)}, u32[]{:S(2)}, u32[]{:S(2)}) collective-permute-start(bf16[272,512]{1,0:T(8,128)(2,1)S(1)} %get-tuple-element.34), channel_id=1, source_target_pairs={{0,8},{4,12},{1,9},{5,13},{2,10},{6,14},{3,11},{7,15}} | collective-permute-start | bytes 835592 | tf_op jit(solution)/shard_map/ppermute | solution.py:248
  118.6 6.7 %collective-permute-start.17 = (bf16[272,512]{1,0:T(8,128)(2,1)S(1)}, bf16[272,512]{1,0:T(8,128)(2,1)S(1)}, u32[]{:S(2)}, u32[]{:S(2)}) collective-permute-start(bf16[272,512]{1,0:T(8,128)(2,1)S(1)} %get-tuple-element.35), channel_id=1, source_target_pairs={{24,16},{28,20},{25,17},{29,21},{26,18},{30,22},{27,19},{31,23}} | collective-permute-start | bytes 835592 | tf_op jit(solution)/shard_map/ppermute | solution.py:257
  120.1 14.5 %collective-permute-start.11 = (bf16[272,512]{1,0:T(8,128)(2,1)}, bf16[272,512]{1,0:T(8,128)(2,1)}, u32[]{:S(2)}, u32[]{:S(2)}) collective-permute-start(bf16[272,512]{1,0:T(8,128)(2,1)} %get-tuple-element.39), channel_id=1, source_target_pairs={{16,8},{20,12},{24,16},{28,20},{17,9},{21,13},{25,17},{29,21},{18,... | collective-permute-start | bytes 835592 | tf_op jit(solution)/shard_map/ppermute | solution.py:257
  121.5 13.2 %collective-permute-start.8 = (bf16[272,512]{1,0:T(8,128)(2,1)S(1)}, bf16[272,512]{1,0:T(8,128)(2,1)}, u32[]{:S(2)}, u32[]{:S(2)}) collective-permute-start(bf16[272,512]{1,0:T(8,128)(2,1)S(1)} %get-tuple-element.38), channel_id=1, source_target_pairs={{0,8},{4,12},{8,16},{12,20},{1,9},{5,13},{9,17},{13,21},{2,10},{6,... | collective-permute-start | bytes 835592 | tf_op jit(solution)/shard_map/ppermute | solution.py:248
  126.2 16.9 %collective-permute-start.15 = (bf16[272,512]{1,0:T(8,128)(2,1)}, bf16[272,512]{1,0:T(8,128)(2,1)}, u32[]{:S(2)}, u32[]{:S(2)}) collective-permute-start(bf16[272,512]{1,0:T(8,128)(2,1)} %get-tuple-element.32), channel_id=1, source_target_pairs={{0,8},{4,12},{8,16},{12,20},{1,9},{5,13},{9,17},{13,21},{2,10},{6,... | collective-permute-start | bytes 835592 | tf_op jit(solution)/shard_map/ppermute | solution.py:248
  131.3 11.8 %collective-permute-start.18 = (bf16[272,512]{1,0:T(8,128)(2,1)}, bf16[272,512]{1,0:T(8,128)(2,1)}, u32[]{:S(2)}, u32[]{:S(2)}) collective-permute-start(bf16[272,512]{1,0:T(8,128)(2,1)} %get-tuple-element.33), channel_id=1, source_target_pairs={{16,8},{20,12},{24,16},{28,20},{17,9},{21,13},{25,17},{29,21},{18,... | collective-permute-start | bytes 835592 | tf_op jit(solution)/shard_map/ppermute | solution.py:257
  136.5 12.4 %collective-permute-start.12 = (bf16[272,512]{1,0:T(8,128)(2,1)}, bf16[272,512]{1,0:T(8,128)(2,1)}, u32[]{:S(2)}, u32[]{:S(2)}) collective-permute-start(bf16[272,512]{1,0:T(8,128)(2,1)} %get-tuple-element.37), channel_id=1, source_target_pairs={{8,0},{12,4},{16,8},{20,12},{24,16},{28,20},{9,1},{13,5},{17,9},{2... | collective-permute-start | bytes 835592 | tf_op jit(solution)/shard_map/ppermute | solution.py:257
  137.8 11.1 %collective-permute-start.9 = (bf16[272,512]{1,0:T(8,128)(2,1)S(1)}, bf16[272,512]{1,0:T(8,128)(2,1)}, u32[]{:S(2)}, u32[]{:S(2)}) collective-permute-start(bf16[272,512]{1,0:T(8,128)(2,1)S(1)} %get-tuple-element.36), channel_id=1, source_target_pairs={{0,8},{4,12},{8,16},{12,20},{16,24},{20,28},{1,9},{5,13},{9,17},{1... | collective-permute-start | bytes 835592 | tf_op jit(solution)/shard_map/ppermute | solution.py:248
  145.1 6.0 %collective-permute-start.16 = (bf16[272,512]{1,0:T(8,128)(2,1)}, bf16[272,512]{1,0:T(8,128)(2,1)}, u32[]{:S(2)}, u32[]{:S(2)}) collective-permute-start(bf16[272,512]{1,0:T(8,128)(2,1)} %get-tuple-element.30), channel_id=1, source_target_pairs={{0,8},{4,12},{8,16},{12,20},{16,24},{20,28},{1,9},{5,13},{9,17},{1... | collective-permute-start | bytes 835592 | tf_op jit(solution)/shard_map/ppermute | solution.py:248
  147.1 8.7 %collective-permute-start.19 = (bf16[272,512]{1,0:T(8,128)(2,1)}, bf16[272,512]{1,0:T(8,128)(2,1)}, u32[]{:S(2)}, u32[]{:S(2)}) collective-permute-start(bf16[272,512]{1,0:T(8,128)(2,1)} %get-tuple-element.31), channel_id=1, source_target_pairs={{8,0},{12,4},{16,8},{20,12},{24,16},{28,20},{9,1},{13,5},{17,9},{2... | collective-permute-start | bytes 835592 | tf_op jit(solution)/shard_map/ppermute | solution.py:257
  163.3 6.1 %collective-permute-start.21 = (bf16[256,1280]{1,0:T(8,128)(2,1)S(1)}, bf16[256,1280]{1,0:T(8,128)(2,1)S(1)}, u32[]{:S(2)}, u32[]{:S(2)}) collective-permute-start(bf16[256,1280]{1,0:T(8,128)(2,1)S(1)} %fusion.4), channel_id=1, source_target_pairs={{0,1},{1,0},{2,3},{3,2},{4,5},{5,4},{6,7},{7,6},{8,9},{9,8},{10,11... | collective-permute-start | bytes 1966088 | tf_op jit(solution)/shard_map/ppermute | solution.py:353
  167.1 9.6 %collective-permute-start.20 = (bf16[256,1280]{1,0:T(8,128)(2,1)S(1)}, bf16[256,1280]{1,0:T(8,128)(2,1)S(1)}, u32[]{:S(2)}, u32[]{:S(2)}) collective-permute-start(bf16[256,1280]{1,0:T(8,128)(2,1)S(1)} %fusion.3), channel_id=1, source_target_pairs={{0,1},{1,0},{2,3},{3,2},{4,5},{5,4},{6,7},{7,6},{8,9},{9,8},{10,11... | collective-permute-start | bytes 1966088 | tf_op jit(solution)/shard_map/ppermute | solution.py:358
  171.3 16.7 %collective-permute-start.22 = (bf16[256,1280]{1,0:T(8,128)(2,1)S(1)}, bf16[256,1280]{1,0:T(8,128)(2,1)S(1)}, u32[]{:S(2)}, u32[]{:S(2)}) collective-permute-start(bf16[256,1280]{1,0:T(8,128)(2,1)S(1)} %add_convert_fusion.1), channel_id=1, source_target_pairs={{0,2},{1,3},{2,0},{3,1},{4,6},{5,7},{6,4},{7,5},{8,10},{9,11},{10,... | collective-permute-start | bytes 1966088 | tf_op jit(solution)/shard_map/ppermute | solution.py:356
  (26 other events, 163.7 us)
